TPU v7x, 32 devices: a whole 2x2x4 slice. The times are simulated.
32 devices in a mesh: gx: 8 (over z, y), gy: 4 (over x, core).
Axes of the slice: x: 2, y: 2, z: 4, core: 2. Of those that a mesh axis runs over, the one named last changes fastest.
Arguments:
- field: float32 [32, 32, 64, 128], P(None, 'gx', 'gy'), may hold values from -6 to 6
- rates: float32 [32], replicated, may hold values from 0.2 to 1
- mixing: float32 [32, 32], replicated, may hold values from -1 to 1
- secretion: float32 [32, 8, 16, 256], P(None, 'gx', 'gy'), may hold values from -6 to 6
- positions: float32 [3, 8, 16, 256], P(None, 'gx', 'gy'), may hold values from 0 to 128, as said below
- stiffness: float32 [8, 16, 256], P('gx', 'gy'), may hold values from 0.5 to 2
- occupancy: int32 [8, 16, 256], P('gx', 'gy'), may hold values from 0 to 1
- offsets: int32 [8, 16, 256], P('gx', 'gy'), may hold values from 0 to 127
- migrant_state: float32 [8, 280, 512], P(None, 'gx', 'gy'), may hold values from -6 to 6
- migrant_live: int32 [8, 8, 512], P(None, 'gx', 'gy'), may hold values 0 or 1
Outputs:
- new_field: float32 [32, 32, 64, 128], P(None, 'gx', 'gy')
- displacement: float32 [3, 8, 16, 256], P(None, 'gx', 'gy')
- arrived: float32 [8, 280, 512], P(None, 'gx', 'gy')
Inputs may be any that keep to these rules, and one draw needn't show every extreme that they name: `positions`: a slot's coordinates lie inside the box of its bin.
All inputs are finite; a program needn't handle non-finite values. No bound on the sum of `migrant_live` on one device may be relied on, other than what follows from the above.
Results may differ from a plain program's by a relative error of at most 0.0003.
Values sent between devices are 32-bit elements; how exact they have to be, the bound alone decides.
A program may use at most 64 MiB of HBM per device.

v0:
```python
import jax
import jax.numpy as jnp
from jax import lax
from jax.sharding import PartitionSpec as P

BIN_XY = 4
BIN_Z = 8
SLOTS = 16
SUBSTEPS = 4


time_step = 0.15
move_step = 0.1
spread_sq = 8.0
shifts = ((-1, -1), (-1, 0), (-1, 1), (0, -1), (0, 1), (1, -1), (1, 0), (1, 1))


def padded_2(cells, sides, width):
    for axis, dim in sides:
        count = lax.axis_size(axis)
        ends = count - 1
        head = lax.slice_in_dim(cells, 0, width, axis=dim)
        tail = lax.slice_in_dim(cells, cells.shape[dim] - width, cells.shape[dim], axis=dim)
        cells = jnp.concatenate(
            [
                lax.ppermute(tail, axis, [(i, (i + 1) % count) for i in range(ends)]),
                cells,
                lax.ppermute(head, axis, [((i + 1) % count, i) for i in range(ends)]),
            ],
            axis=dim,
        )
    return cells


def shifted(block, axis, distance):
    devices = range(lax.axis_size(axis))
    route = [(i - distance, i) for i in devices if i - distance in devices]
    return lax.ppermute(block, axis, route)


def advance(padded, source, rates, mixing):
    center = padded[:, 1:-1, 1:-1, :]
    deeper = jnp.pad(center, ((0, 0), (0, 0), (0, 0), (1, 1)))
    beside = padded[:, 2:, 1:-1, :] + padded[:, :-2, 1:-1, :]
    beside = beside + padded[:, 1:-1, 2:, :] + padded[:, 1:-1, :-2, :]
    beside = beside + deeper[:, :, :, 2:] + deeper[:, :, :, :-2]
    laplace = beside - 6.0 * center
    species = center.shape[0]
    mixed = jnp.dot(mixing, center.reshape(species, -1), precision=lax.Precision.HIGHEST).reshape(
        center.shape
    )
    return (
        center
        + time_step * (rates[:, None, None, None] * laplace)
        + time_step * mixed
        + time_step * source
    )


def deposit(secretion, occupancy, offsets):
    species, bins_x, bins_y, lanes = secretion.shape
    layers = lanes // SLOTS
    cells = BIN_XY * BIN_XY * BIN_Z
    count = bins_x * bins_y * layers
    rates_slot = secretion.reshape(species, count, SLOTS)
    place = offsets.reshape(count, SLOTS)
    alive = occupancy.reshape(count, SLOTS).astype(jnp.float32)
    voxel_ids = lax.broadcasted_iota(jnp.int32, (count, SLOTS, cells), 2)
    onehot = (place[:, :, None] == voxel_ids).astype(jnp.float32) * alive[:, :, None]
    filled = jnp.einsum("snk,nkc->snc", rates_slot, onehot, precision=lax.Precision.HIGHEST)
    filled = filled.reshape(species, bins_x, bins_y, layers, BIN_XY, BIN_XY, BIN_Z)
    filled = jnp.transpose(filled, (0, 1, 4, 2, 5, 3, 6))
    return filled.reshape(species, bins_x * BIN_XY, bins_y * BIN_XY, layers * BIN_Z)


def pair_forces(points, padded, occupancy):
    planes, bins_x, bins_y, lanes = points.shape
    layers = lanes // SLOTS
    boxed = padded.reshape(planes, bins_x + 2, bins_y + 2, layers, SLOTS)
    boxed = jnp.pad(boxed, ((0, 0), (0, 0), (0, 0), (1, 1), (0, 0)))
    owned = points.reshape(planes, bins_x, bins_y, layers, SLOTS)[:3, :, :, :, :, None]
    force = jnp.zeros((3, bins_x, bins_y, layers, SLOTS), jnp.float32)
    for offset_x in range(3):
        nearby = jnp.concatenate(
            [
                boxed[
                    :,
                    offset_x : offset_x + bins_x,
                    offset_y : offset_y + bins_y,
                    offset_z : offset_z + layers,
                    :,
                ]
                for offset_y in range(3)
                for offset_z in range(3)
            ],
            axis=-1,
        )
        apart = owned - nearby[:3, :, :, :, None, :]
        strength = nearby[3][:, :, :, None, :] * jnp.exp(
            -jnp.sum(apart * apart, axis=0) / spread_sq
        )
        force = force + jnp.sum(apart * strength[None], axis=-1)
    active = occupancy.reshape(1, bins_x, bins_y, layers, SLOTS).astype(jnp.float32)
    return (move_step * active * force).reshape(3, bins_x, bins_y, lanes)


def on_device(
    field,
    rates,
    mixing,
    secretion,
    positions,
    stiffness,
    occupancy,
    offsets,
    migrant_state,
    migrant_live,
):
    weight = stiffness * occupancy.astype(jnp.float32)
    points = jnp.concatenate([positions, weight[None]], axis=0)
    bordered = padded_2(points, (("gx", 1), ("gy", 2)), 1)
    payload = migrant_state * migrant_live.astype(jnp.float32)
    moving = [payload[index] for index in range(8)]
    for stride in (1, -1):
        picked = [index for index in range(8) if shifts[index][0] == stride]
        landed = shifted(jnp.stack([moving[index] for index in picked]), "gx", stride)
        for place, index in enumerate(picked):
            moving[index] = landed[place]
    for stride in (1, -1):
        picked = [index for index in range(8) if shifts[index][1] == stride]
        landed = shifted(jnp.stack([moving[index] for index in picked]), "gy", stride)
        for place, index in enumerate(picked):
            moving[index] = landed[place]
    arrived = jnp.stack(moving)
    source = deposit(secretion, occupancy, offsets)
    current = field
    for substep in range(SUBSTEPS):
        padded = padded_2(current, (("gx", 1), ("gy", 2)), 1)
        current = advance(padded, source, rates, mixing)
    displacement = pair_forces(points, bordered, occupancy)
    return (current, displacement, arrived)


def solution(mesh):
    return jax.shard_map(
        on_device,
        mesh=mesh,
        in_specs=(
            P(None, "gx", "gy", None),
            P(),
            P(),
            P(None, "gx", "gy", None),
            P(None, "gx", "gy", None),
            P("gx", "gy", None),
            P("gx", "gy", None),
            P("gx", "gy", None),
            P(None, "gx", "gy"),
            P(None, "gx", "gy"),
        ),
        out_specs=(P(None, "gx", "gy", None), P(None, "gx", "gy", None), P(None, "gx", "gy")),
        check_vma=False,
    )
```

profile of v0, /device:TPU:1, one launch (start us, length us, event | category | flops | bytes accessed | tf_op | source)
XLA Modules:
  0.0 156.4 jit_solution(14033247223056270267)
XLA Ops:
  3.5 4.6 %collective-permute-start.16 = (f32[4,1,4,256]{3,2,1,0:T(4,128)S(1)}, f32[4,1,4,256]{3,2,1,0:T(4,128)S(1)}, u32[]{:S(2)}, u32[]{:S(2)}) collective-permute-start(f32[4,1,4,256]{3,2,1,0:T(4,128)S(1)} %pad_maximum_fusion.40), channel_id=1, source_target_pairs={{0,4},{4,8},{8,12},{12,16},{16,20},{20,24},{24,28},{1,5},{5,9},{9,... | collective-permute-start | bytes 49160 | tf_op jit(solution)/shard_map/ppermute | solution.py:26
  8.1 1.8 %copy.87 = f32[32,4,16,128]{3,0,2,1:T(8,128)S(1)} copy(f32[32,4,16,128]{3,2,1,0:T(8,128)} %param.10) | data formatting | bytes 2097152 | tf_op args[0]
  10.8 5.0 %collective-permute-start.1 = (f32[32,1,16,128]{3,0,2,1:T(8,128)}, f32[32,1,16,128]{3,0,2,1:T(8,128)}, u32[]{:S(2)}, u32[]{:S(2)}) collective-permute-start(f32[32,1,16,128]{3,0,2,1:T(8,128)} %get-tuple-element.35), channel_id=1, source_target_pairs={{0,4},{4,8},{8,12},{12,16},{16,20},{20,24},{24,28},{1,5},{5,9},{9,... | collective-permute-start | bytes 786440 | tf_op jit(solution)/shard_map/ppermute | solution.py:26
  19.5 2.2 %fusion.9 = f32[32,64,128]{2,0,1:T(8,128)S(1)} fusion(f32[32,64,16]{0,2,1:T(8,128)S(1)} %bitcast.97, f32[64,16]{1,0:T(8,128)S(1)} %convert_element_type.30, s32[64,16]{1,0:T(8,128)S(1)} %eq.10), kind=kOutput, calls=%fused_computation.45 | convolution fusion | flops 50855936 | bytes 1187840 | tf_op jit(solution)/shard_map/snk,nkc->snc/dot_general | solution.py:70
  21.8 3.4 %collective-permute-start.19 = (f32[4,3,1,256]{3,2,1,0:T(1,128)S(1)}, f32[4,3,1,256]{3,2,1,0:T(1,128)S(1)}, u32[]{:S(2)}, u32[]{:S(2)}) collective-permute-start(f32[4,3,1,256]{3,2,1,0:T(1,128)S(1)} %get-tuple-element.72), channel_id=1, source_target_pairs={{1,0},{2,1},{3,2},{5,4},{6,5},{7,6},{9,8},{10,9},{11,10},{13,12},{... | collective-permute-start | bytes 36872 | tf_op jit(solution)/shard_map/ppermute | solution.py:28
  25.2 3.0 %collective-permute-start.18 = (f32[4,3,1,256]{3,2,1,0:T(1,128)S(1)}, f32[4,3,1,256]{3,2,1,0:T(1,128)S(1)}, u32[]{:S(2)}, u32[]{:S(2)}) collective-permute-start(f32[4,3,1,256]{3,2,1,0:T(1,128)S(1)} %get-tuple-element.71), channel_id=1, source_target_pairs={{0,1},{1,2},{2,3},{4,5},{5,6},{6,7},{8,9},{9,10},{10,11},{12,13},{... | collective-permute-start | bytes 36872 | tf_op jit(solution)/shard_map/ppermute | solution.py:26
  28.9 2.7 %copy.90 = f32[32,64,128]{0,2,1:T(8,128)} copy(f32[32,64,128]{2,0,1:T(8,128)S(1)} %fusion.9) | data formatting | bytes 2097152 | tf_op jit(solution)/shard_map/mul | solution.py:56
  31.6 4.8 %copy.91 = f32[32,1,4,4,4,16,8]{0,6,5,4,3,2,1:T(8,128)} copy(f32[32,1,4,4,4,16,8]{0,6,4,2,5,3,1:T(8,128)} %bitcast.88) | data formatting | bytes 2097152 | tf_op jit(solution)/shard_map/mul | solution.py:56
  36.4 2.9 %copy.92 = f32[32,4,16,128]{3,0,2,1:T(8,128)S(1)} copy(f32[32,4,16,128]{0,3,2,1:T(8,128)} %bitcast.89) | data formatting | bytes 2097152 | tf_op jit(solution)/shard_map/mul | solution.py:56
  41.0 5.5 %collective-permute-start.21 = (f32[3,35,128]{2,1,0:T(8,128)}, f32[3,35,128]{2,1,0:T(8,128)}, u32[]{:S(2)}, u32[]{:S(2)}) collective-permute-start(f32[3,35,128]{2,1,0:T(8,128)} %get-tuple-element.66), channel_id=1, source_target_pairs={{0,4},{4,8},{8,12},{12,16},{16,20},{20,24},{24,28},{1,5},{5,9},{9,... | collective-permute-start | bytes 161288 | tf_op jit(solution)/shard_map/ppermute | solution.py:38
  56.3 2.0 %fusion.3 = (f32[3,4,16,16]{3,2,1,0:T(8,128)S(1)}, f32[4,16,16,144]{3,2,1,0:T(8,128)S(1)}, f32[3,4,16,16]{3,2,1,0:T(8,128)S(1)}) fusion(f32[4,16,16,144]{3,2,1,0:T(8,128)S(1)} %get-tuple-element.75, f32[3,4,16,16]{3,2,1,0:T(8,128)S(1)} %sub.95, f32[4,16,16,144]{3,2,1,0:T(8,128)S(1)} %get-tuple-element.76, f32[4,1,4,16,144]{4,3,0,2,1:T(8,128)S(1)} %concatenate.107, ...), kind=kLoop, calls=%fused_computation.12 | loop fusion | flops 3827712 | bytes 3399680 | tf_op jit(solution)/shard_map/reduce_sum | solution.py:102
  62.0 1.9 %collective-permute-start.22 = (f32[3,35,128]{2,1,0:T(8,128)S(1)}, f32[3,35,128]{2,1,0:T(8,128)S(1)}, u32[]{:S(2)}, u32[]{:S(2)}) collective-permute-start(f32[3,35,128]{2,1,0:T(8,128)S(1)} %pad_maximum_fusion.38), channel_id=1, source_target_pairs={{1,0},{2,1},{3,2},{5,4},{6,5},{7,6},{9,8},{10,9},{11,10},{13,12},{... | collective-permute-start | bytes 161288 | tf_op jit(solution)/shard_map/ppermute | solution.py:38
  64.5 3.0 %collective-permute-done.22 = f32[3,35,128]{2,1,0:T(8,128)S(1)} collective-permute-done((f32[3,35,128]{2,1,0:T(8,128)S(1)}, f32[3,35,128]{2,1,0:T(8,128)S(1)}, u32[]{:S(2)}, u32[]{:S(2)}) %collective-permute-start.22) | collective-permute-done | bytes 53792 | tf_op jit(solution)/shard_map/ppermute | solution.py:38
  70.9 1.9 %collective-permute-start.3 = (f32[32,6,1,128]{3,0,2,1:T(8,128)S(1)}, f32[32,6,1,128]{3,0,2,1:T(8,128)S(1)}, u32[]{:S(2)}, u32[]{:S(2)}) collective-permute-start(f32[32,6,1,128]{3,0,2,1:T(8,128)S(1)} %get-tuple-element.27), channel_id=1, source_target_pairs={{0,1},{1,2},{2,3},{4,5},{5,6},{6,7},{8,9},{9,10},{10,11},{12,13},{... | collective-permute-start | bytes 294920 | tf_op jit(solution)/shard_map/ppermute | solution.py:26
  72.8 2.4 %collective-permute-start.2 = (f32[32,6,1,128]{3,0,2,1:T(8,128)S(1)}, f32[32,6,1,128]{3,0,2,1:T(8,128)S(1)}, u32[]{:S(2)}, u32[]{:S(2)}) collective-permute-start(f32[32,6,1,128]{3,0,2,1:T(8,128)S(1)} %get-tuple-element.26), channel_id=1, source_target_pairs={{1,0},{2,1},{3,2},{5,4},{6,5},{7,6},{9,8},{10,9},{11,10},{13,12},{... | collective-permute-start | bytes 294920 | tf_op jit(solution)/shard_map/ppermute | solution.py:28
  75.2 3.3 %collective-permute-start.23 = (f32[3,35,128]{2,1,0:T(8,128)S(1)}, f32[3,35,128]{2,1,0:T(8,128)S(1)}, u32[]{:S(2)}, u32[]{:S(2)}) collective-permute-start(f32[3,35,128]{2,1,0:T(8,128)S(1)} %pad_maximum_fusion.39), channel_id=1, source_target_pairs={{0,1},{1,2},{2,3},{4,5},{5,6},{6,7},{8,9},{9,10},{10,11},{12,13},{... | collective-permute-start | bytes 161288 | tf_op jit(solution)/shard_map/ppermute | solution.py:38
  78.8 3.0 %fusion.11 = f32[32,4,16,128]{3,0,2,1:T(8,128)S(1)} fusion(f32[32,4,16,128]{3,0,2,1:T(8,128)S(1)} %copy.92, f32[32,4,16,128]{3,0,2,1:T(8,128)S(1)} %copy-done.3, f32[32,6,16,128]{3,0,2,1:T(8,128)S(1)} %constant_dynamic-update-slice_fusion, f32[32,6,1,128]{3,0,2,1:T(8,128)S(1)} %collective-permute-done.3, f32[32,6,1,128]{3,0,2,1:T(8,128)S(1)} %collective-permute-done.2, ...), kind=kOutput, calls=%fused_computation.48 | convolution fusion | flops 105119744 | bytes 6492288 | tf_op jit(solution)/shard_map/dot_general | solution.py:49
  83.1 4.6 %collective-permute-start.5 = (f32[32,1,16,128]{3,0,2,1:T(8,128)S(1)}, f32[32,1,16,128]{3,0,2,1:T(8,128)S(1)}, u32[]{:S(2)}, u32[]{:S(2)}) collective-permute-start(f32[32,1,16,128]{3,0,2,1:T(8,128)S(1)} %get-tuple-element.32), channel_id=1, source_target_pairs={{0,4},{4,8},{8,12},{12,16},{16,20},{20,24},{24,28},{1,5},{5,9},{9,... | collective-permute-start | bytes 786440 | tf_op jit(solution)/shard_map/ppermute | solution.py:26
  88.4 3.3 %collective-permute-done.4 = f32[32,1,16,128]{3,0,2,1:T(8,128)S(1)} collective-permute-done((f32[32,1,16,128]{3,0,2,1:T(8,128)S(1)}, f32[32,1,16,128]{3,0,2,1:T(8,128)S(1)}, u32[]{:S(2)}, u32[]{:S(2)}) %collective-permute-start.4) | collective-permute-done | bytes 262176 | tf_op jit(solution)/shard_map/ppermute | solution.py:28
  91.7 6.4 %collective-permute-done.5 = f32[32,1,16,128]{3,0,2,1:T(8,128)S(1)} collective-permute-done((f32[32,1,16,128]{3,0,2,1:T(8,128)S(1)}, f32[32,1,16,128]{3,0,2,1:T(8,128)S(1)}, u32[]{:S(2)}, u32[]{:S(2)}) %collective-permute-start.5) | collective-permute-done | bytes 262176 | tf_op jit(solution)/shard_map/ppermute | solution.py:26
  98.1 1.9 %collective-permute-start.7 = (f32[32,6,1,128]{3,0,2,1:T(8,128)S(1)}, f32[32,6,1,128]{3,0,2,1:T(8,128)S(1)}, u32[]{:S(2)}, u32[]{:S(2)}) collective-permute-start(f32[32,6,1,128]{3,0,2,1:T(8,128)S(1)} %get-tuple-element.25), channel_id=1, source_target_pairs={{0,1},{1,2},{2,3},{4,5},{5,6},{6,7},{8,9},{9,10},{10,11},{12,13},{... | collective-permute-start | bytes 294920 | tf_op jit(solution)/shard_map/ppermute | solution.py:26
  100.0 2.4 %collective-permute-start.6 = (f32[32,6,1,128]{3,0,2,1:T(8,128)S(1)}, f32[32,6,1,128]{3,0,2,1:T(8,128)S(1)}, u32[]{:S(2)}, u32[]{:S(2)}) collective-permute-start(f32[32,6,1,128]{3,0,2,1:T(8,128)S(1)} %get-tuple-element.24), channel_id=1, source_target_pairs={{1,0},{2,1},{3,2},{5,4},{6,5},{7,6},{9,8},{10,9},{11,10},{13,12},{... | collective-permute-start | bytes 294920 | tf_op jit(solution)/shard_map/ppermute | solution.py:28
  108.4 4.7 %collective-permute-start.9 = (f32[32,1,16,128]{3,0,2,1:T(8,128)S(1)}, f32[32,1,16,128]{3,0,2,1:T(8,128)S(1)}, u32[]{:S(2)}, u32[]{:S(2)}) collective-permute-start(f32[32,1,16,128]{3,0,2,1:T(8,128)S(1)} %get-tuple-element.30), channel_id=1, source_target_pairs={{0,4},{4,8},{8,12},{12,16},{16,20},{20,24},{24,28},{1,5},{5,9},{9,... | collective-permute-start | bytes 786440 | tf_op jit(solution)/shard_map/ppermute | solution.py:26
  113.7 1.9 %collective-permute-done.8 = f32[32,1,16,128]{3,0,2,1:T(8,128)S(1)} collective-permute-done((f32[32,1,16,128]{3,0,2,1:T(8,128)S(1)}, f32[32,1,16,128]{3,0,2,1:T(8,128)S(1)}, u32[]{:S(2)}, u32[]{:S(2)}) %collective-permute-start.8) | collective-permute-done | bytes 262176 | tf_op jit(solution)/shard_map/ppermute | solution.py:28
  115.6 6.4 %collective-permute-done.9 = f32[32,1,16,128]{3,0,2,1:T(8,128)S(1)} collective-permute-done((f32[32,1,16,128]{3,0,2,1:T(8,128)S(1)}, f32[32,1,16,128]{3,0,2,1:T(8,128)S(1)}, u32[]{:S(2)}, u32[]{:S(2)}) %collective-permute-start.9) | collective-permute-done | bytes 262176 | tf_op jit(solution)/shard_map/ppermute | solution.py:26
  122.1 1.9 %collective-permute-start.11 = (f32[32,6,1,128]{3,0,2,1:T(8,128)S(1)}, f32[32,6,1,128]{3,0,2,1:T(8,128)S(1)}, u32[]{:S(2)}, u32[]{:S(2)}) collective-permute-start(f32[32,6,1,128]{3,0,2,1:T(8,128)S(1)} %get-tuple-element.23), channel_id=1, source_target_pairs={{0,1},{1,2},{2,3},{4,5},{5,6},{6,7},{8,9},{9,10},{10,11},{12,13},{... | collective-permute-start | bytes 294920 | tf_op jit(solution)/shard_map/ppermute | solution.py:26
  124.0 2.4 %collective-permute-start.10 = (f32[32,6,1,128]{3,0,2,1:T(8,128)S(1)}, f32[32,6,1,128]{3,0,2,1:T(8,128)S(1)}, u32[]{:S(2)}, u32[]{:S(2)}) collective-permute-start(f32[32,6,1,128]{3,0,2,1:T(8,128)S(1)} %get-tuple-element.22), channel_id=1, source_target_pairs={{1,0},{2,1},{3,2},{5,4},{6,5},{7,6},{9,8},{10,9},{11,10},{13,12},{... | collective-permute-start | bytes 294920 | tf_op jit(solution)/shard_map/ppermute | solution.py:28
  132.3 4.6 %collective-permute-start.13 = (f32[32,1,16,128]{3,0,2,1:T(8,128)S(1)}, f32[32,1,16,128]{3,0,2,1:T(8,128)S(1)}, u32[]{:S(2)}, u32[]{:S(2)}) collective-permute-start(f32[32,1,16,128]{3,0,2,1:T(8,128)S(1)} %get-tuple-element.28), channel_id=1, source_target_pairs={{0,4},{4,8},{8,12},{12,16},{16,20},{20,24},{24,28},{1,5},{5,9},{9,... | collective-permute-start | bytes 786440 | tf_op jit(solution)/shard_map/ppermute | solution.py:26
  139.4 6.4 %collective-permute-done.13 = f32[32,1,16,128]{3,0,2,1:T(8,128)S(1)} collective-permute-done((f32[32,1,16,128]{3,0,2,1:T(8,128)S(1)}, f32[32,1,16,128]{3,0,2,1:T(8,128)S(1)}, u32[]{:S(2)}, u32[]{:S(2)}) %collective-permute-start.13) | collective-permute-done | bytes 262176 | tf_op jit(solution)/shard_map/ppermute | solution.py:26
  145.8 1.9 %collective-permute-start.15 = (f32[32,6,1,128]{3,0,2,1:T(8,128)S(1)}, f32[32,6,1,128]{3,0,2,1:T(8,128)S(1)}, u32[]{:S(2)}, u32[]{:S(2)}) collective-permute-start(f32[32,6,1,128]{3,0,2,1:T(8,128)S(1)} %get-tuple-element.21), channel_id=1, source_target_pairs={{0,1},{1,2},{2,3},{4,5},{5,6},{6,7},{8,9},{9,10},{10,11},{12,13},{... | collective-permute-start | bytes 294920 | tf_op jit(solution)/shard_map/ppermute | solution.py:26
  147.8 2.6 %collective-permute-start.14 = (f32[32,6,1,128]{3,0,2,1:T(8,128)S(1)}, f32[32,6,1,128]{3,0,2,1:T(8,128)S(1)}, u32[]{:S(2)}, u32[]{:S(2)}) collective-permute-start(f32[32,6,1,128]{3,0,2,1:T(8,128)S(1)} %get-tuple-element.20), channel_id=1, source_target_pairs={{1,0},{2,1},{3,2},{5,4},{6,5},{7,6},{9,8},{10,9},{11,10},{13,12},{... | collective-permute-start | bytes 294920 | tf_op jit(solution)/shard_map/ppermute | solution.py:28
  150.4 1.7 %fusion.8 = f32[4,8,64,128]{3,1,2,0:T(8,128)S(1)} fusion(f32[32,32]{1,0:T(8,128)S(1)} %copy-done, f32[4,8,64,128]{3,2,1,0:T(8,128)S(1)} %bitcast.96), kind=kOutput, calls=%fused_computation.43 | convolution fusion | flops 100925440 | bytes 2101248 | tf_op jit(solution)/shard_map/dot_general | solution.py:49
  (120 shorter events, 48.4 us)
Async XLA Ops:
  0.6 78.1 %copy-start = (f32[32,32]{1,0:T(8,128)S(1)}, f32[32,32]{1,0:T(8,128)}, u32[]{:S(2)}) copy-start(f32[32,32]{1,0:T(8,128)} %param.12) | copy-start | bytes 12292
  0.6 18.5 %copy-start.9 = (s32[1,4,256]{2,1,0:T(4,128)S(1)}, s32[1,4,256]{2,1,0:T(4,128)}, u32[]{:S(2)}) copy-start(s32[1,4,256]{2,1,0:T(4,128)} %param.16) | copy-start | bytes 12292
  0.7 21.1 %copy-start.6 = (f32[3,1,4,256]{3,2,1,0:T(4,128)S(1)}, f32[3,1,4,256]{3,2,1,0:T(4,128)}, u32[]{:S(2)}) copy-start(f32[3,1,4,256]{3,2,1,0:T(4,128)} %param.14) | copy-start | bytes 36868
  0.7 18.5 %copy-start.8 = (f32[32,1,4,256]{3,2,1,0:T(4,128)S(1)}, f32[32,1,4,256]{3,2,1,0:T(4,128)}, u32[]{:S(2)}) copy-start(f32[32,1,4,256]{3,2,1,0:T(4,128)} %param.13) | copy-start | bytes 393220
  0.7 18.8 %copy-start.11 = (s32[1,4,256]{2,1,0:T(4,128)S(1)}, s32[1,4,256]{2,1,0:T(4,128)}, u32[]{:S(2)}) copy-start(s32[1,4,256]{2,1,0:T(4,128)} %param.17) | copy-start | bytes 12292
  2.2 19.5 %collective-permute-start.17 = (f32[4,1,4,256]{3,2,1,0:T(4,128)S(1)}, f32[4,1,4,256]{3,2,1,0:T(4,128)S(1)}, u32[]{:S(2)}, u32[]{:S(2)}) collective-permute-start(f32[4,1,4,256]{3,2,1,0:T(4,128)S(1)} %pad_maximum_fusion.40), channel_id=1, source_target_pairs={{4,0},{8,4},{12,8},{16,12},{20,16},{24,20},{28,24},{5,1},{9,5},{13... | collective-permute-start | bytes 49160 | tf_op jit(solution)/shard_map/ppermute | solution.py:28
  3.5 18.2 %collective-permute-start.16 = (f32[4,1,4,256]{3,2,1,0:T(4,128)S(1)}, f32[4,1,4,256]{3,2,1,0:T(4,128)S(1)}, u32[]{:S(2)}, u32[]{:S(2)}) collective-permute-start(f32[4,1,4,256]{3,2,1,0:T(4,128)S(1)} %pad_maximum_fusion.40), channel_id=1, source_target_pairs={{0,4},{4,8},{8,12},{12,16},{16,20},{20,24},{24,28},{1,5},{5,9},{9,... | collective-permute-start | bytes 49160 | tf_op jit(solution)/shard_map/ppermute | solution.py:26
  10.8 57.4 %collective-permute-start.1 = (f32[32,1,16,128]{3,0,2,1:T(8,128)}, f32[32,1,16,128]{3,0,2,1:T(8,128)}, u32[]{:S(2)}, u32[]{:S(2)}) collective-permute-start(f32[32,1,16,128]{3,0,2,1:T(8,128)} %get-tuple-element.35), channel_id=1, source_target_pairs={{0,4},{4,8},{8,12},{12,16},{16,20},{20,24},{24,28},{1,5},{5,9},{9,... | collective-permute-start | bytes 786440 | tf_op jit(solution)/shard_map/ppermute | solution.py:26
  15.8 54.1 %collective-permute-start = (f32[32,1,16,128]{3,0,2,1:T(8,128)}, f32[32,1,16,128]{3,0,2,1:T(8,128)}, u32[]{:S(2)}, u32[]{:S(2)}) collective-permute-start(f32[32,1,16,128]{3,0,2,1:T(8,128)} %get-tuple-element.34), channel_id=1, source_target_pairs={{4,0},{8,4},{12,8},{16,12},{20,16},{24,20},{28,24},{5,1},{9,5},{13... | collective-permute-start | bytes 786440 | tf_op jit(solution)/shard_map/ppermute | solution.py:28
  17.8 42.7 %collective-permute-start.20 = (f32[3,35,128]{2,1,0:T(8,128)}, f32[3,35,128]{2,1,0:T(8,128)}, u32[]{:S(2)}, u32[]{:S(2)}) collective-permute-start(f32[3,35,128]{2,1,0:T(8,128)} %get-tuple-element.65), channel_id=1, source_target_pairs={{4,0},{8,4},{12,8},{16,12},{20,16},{24,20},{28,24},{5,1},{9,5},{13... | collective-permute-start | bytes 161288 | tf_op jit(solution)/shard_map/ppermute | solution.py:38
  21.8 19.3 %collective-permute-start.19 = (f32[4,3,1,256]{3,2,1,0:T(1,128)S(1)}, f32[4,3,1,256]{3,2,1,0:T(1,128)S(1)}, u32[]{:S(2)}, u32[]{:S(2)}) collective-permute-start(f32[4,3,1,256]{3,2,1,0:T(1,128)S(1)} %get-tuple-element.72), channel_id=1, source_target_pairs={{1,0},{2,1},{3,2},{5,4},{6,5},{7,6},{9,8},{10,9},{11,10},{13,12},{... | collective-permute-start | bytes 36872 | tf_op jit(solution)/shard_map/ppermute | solution.py:28
  25.2 21.4 %collective-permute-start.18 = (f32[4,3,1,256]{3,2,1,0:T(1,128)S(1)}, f32[4,3,1,256]{3,2,1,0:T(1,128)S(1)}, u32[]{:S(2)}, u32[]{:S(2)}) collective-permute-start(f32[4,3,1,256]{3,2,1,0:T(1,128)S(1)} %get-tuple-element.71), channel_id=1, source_target_pairs={{0,1},{1,2},{2,3},{4,5},{5,6},{6,7},{8,9},{9,10},{10,11},{12,13},{... | collective-permute-start | bytes 36872 | tf_op jit(solution)/shard_map/ppermute | solution.py:26
  41.0 18.6 %collective-permute-start.21 = (f32[3,35,128]{2,1,0:T(8,128)}, f32[3,35,128]{2,1,0:T(8,128)}, u32[]{:S(2)}, u32[]{:S(2)}) collective-permute-start(f32[3,35,128]{2,1,0:T(8,128)} %get-tuple-element.66), channel_id=1, source_target_pairs={{0,4},{4,8},{8,12},{12,16},{16,20},{20,24},{24,28},{1,5},{5,9},{9,... | collective-permute-start | bytes 161288 | tf_op jit(solution)/shard_map/ppermute | solution.py:38
  58.5 20.2 %copy-start.3 = (f32[32,4,16,128]{3,0,2,1:T(8,128)S(1)}, f32[32,4,16,128]{3,0,2,1:T(8,128)}, u32[]{:S(2)}) copy-start(f32[32,4,16,128]{3,0,2,1:T(8,128)} %copy-done.2) | copy-start | bytes 3145732
  58.6 20.2 %copy-start.10 = (f32[32]{0:T(128)S(1)}, f32[32]{0:T(128)}, u32[]{:S(2)}) copy-start(f32[32]{0:T(128)} %param.11) | copy-start | bytes 388
  59.7 19.1 %copy-start.4 = (f32[4,8,64,128]{3,2,1,0:T(8,128)S(1)}, f32[4,8,64,128]{3,2,1,0:T(8,128)}, u32[]{:S(2)}) copy-start(f32[4,8,64,128]{3,2,1,0:T(8,128)} %copy.112) | copy-start | bytes 3145732
  62.0 5.5 %collective-permute-start.22 = (f32[3,35,128]{2,1,0:T(8,128)S(1)}, f32[3,35,128]{2,1,0:T(8,128)S(1)}, u32[]{:S(2)}, u32[]{:S(2)}) collective-permute-start(f32[3,35,128]{2,1,0:T(8,128)S(1)} %pad_maximum_fusion.38), channel_id=1, source_target_pairs={{1,0},{2,1},{3,2},{5,4},{6,5},{7,6},{9,8},{10,9},{11,10},{13,12},{... | collective-permute-start | bytes 161288 | tf_op jit(solution)/shard_map/ppermute | solution.py:38
  70.9 7.7 %collective-permute-start.3 = (f32[32,6,1,128]{3,0,2,1:T(8,128)S(1)}, f32[32,6,1,128]{3,0,2,1:T(8,128)S(1)}, u32[]{:S(2)}, u32[]{:S(2)}) collective-permute-start(f32[32,6,1,128]{3,0,2,1:T(8,128)S(1)} %get-tuple-element.27), channel_id=1, source_target_pairs={{0,1},{1,2},{2,3},{4,5},{5,6},{6,7},{8,9},{9,10},{10,11},{12,13},{... | collective-permute-start | bytes 294920 | tf_op jit(solution)/shard_map/ppermute | solution.py:26
  72.8 5.9 %collective-permute-start.2 = (f32[32,6,1,128]{3,0,2,1:T(8,128)S(1)}, f32[32,6,1,128]{3,0,2,1:T(8,128)S(1)}, u32[]{:S(2)}, u32[]{:S(2)}) collective-permute-start(f32[32,6,1,128]{3,0,2,1:T(8,128)S(1)} %get-tuple-element.26), channel_id=1, source_target_pairs={{1,0},{2,1},{3,2},{5,4},{6,5},{7,6},{9,8},{10,9},{11,10},{13,12},{... | collective-permute-start | bytes 294920 | tf_op jit(solution)/shard_map/ppermute | solution.py:28
  75.2 12.5 %collective-permute-start.23 = (f32[3,35,128]{2,1,0:T(8,128)S(1)}, f32[3,35,128]{2,1,0:T(8,128)S(1)}, u32[]{:S(2)}, u32[]{:S(2)}) collective-permute-start(f32[3,35,128]{2,1,0:T(8,128)S(1)} %pad_maximum_fusion.39), channel_id=1, source_target_pairs={{0,1},{1,2},{2,3},{4,5},{5,6},{6,7},{8,9},{9,10},{10,11},{12,13},{... | collective-permute-start | bytes 161288 | tf_op jit(solution)/shard_map/ppermute | solution.py:38
  81.8 9.8 %collective-permute-start.4 = (f32[32,1,16,128]{3,0,2,1:T(8,128)S(1)}, f32[32,1,16,128]{3,0,2,1:T(8,128)S(1)}, u32[]{:S(2)}, u32[]{:S(2)}) collective-permute-start(f32[32,1,16,128]{3,0,2,1:T(8,128)S(1)} %get-tuple-element.33), channel_id=1, source_target_pairs={{4,0},{8,4},{12,8},{16,12},{20,16},{24,20},{28,24},{5,1},{9,5},{13... | collective-permute-start | bytes 786440 | tf_op jit(solution)/shard_map/ppermute | solution.py:28
  83.1 14.9 %collective-permute-start.5 = (f32[32,1,16,128]{3,0,2,1:T(8,128)S(1)}, f32[32,1,16,128]{3,0,2,1:T(8,128)S(1)}, u32[]{:S(2)}, u32[]{:S(2)}) collective-permute-start(f32[32,1,16,128]{3,0,2,1:T(8,128)S(1)} %get-tuple-element.32), channel_id=1, source_target_pairs={{0,4},{4,8},{8,12},{12,16},{16,20},{20,24},{24,28},{1,5},{5,9},{9,... | collective-permute-start | bytes 786440 | tf_op jit(solution)/shard_map/ppermute | solution.py:26
  98.1 6.2 %collective-permute-start.7 = (f32[32,6,1,128]{3,0,2,1:T(8,128)S(1)}, f32[32,6,1,128]{3,0,2,1:T(8,128)S(1)}, u32[]{:S(2)}, u32[]{:S(2)}) collective-permute-start(f32[32,6,1,128]{3,0,2,1:T(8,128)S(1)} %get-tuple-element.25), channel_id=1, source_target_pairs={{0,1},{1,2},{2,3},{4,5},{5,6},{6,7},{8,9},{9,10},{10,11},{12,13},{... | collective-permute-start | bytes 294920 | tf_op jit(solution)/shard_map/ppermute | solution.py:26
  100.0 5.9 %collective-permute-start.6 = (f32[32,6,1,128]{3,0,2,1:T(8,128)S(1)}, f32[32,6,1,128]{3,0,2,1:T(8,128)S(1)}, u32[]{:S(2)}, u32[]{:S(2)}) collective-permute-start(f32[32,6,1,128]{3,0,2,1:T(8,128)S(1)} %get-tuple-element.24), channel_id=1, source_target_pairs={{1,0},{2,1},{3,2},{5,4},{6,5},{7,6},{9,8},{10,9},{11,10},{13,12},{... | collective-permute-start | bytes 294920 | tf_op jit(solution)/shard_map/ppermute | solution.py:28
  107.1 8.5 %collective-permute-start.8 = (f32[32,1,16,128]{3,0,2,1:T(8,128)S(1)}, f32[32,1,16,128]{3,0,2,1:T(8,128)S(1)}, u32[]{:S(2)}, u32[]{:S(2)}) collective-permute-start(f32[32,1,16,128]{3,0,2,1:T(8,128)S(1)} %get-tuple-element.31), channel_id=1, source_target_pairs={{4,0},{8,4},{12,8},{16,12},{20,16},{24,20},{28,24},{5,1},{9,5},{13... | collective-permute-start | bytes 786440 | tf_op jit(solution)/shard_map/ppermute | solution.py:28
  108.4 13.7 %collective-permute-start.9 = (f32[32,1,16,128]{3,0,2,1:T(8,128)S(1)}, f32[32,1,16,128]{3,0,2,1:T(8,128)S(1)}, u32[]{:S(2)}, u32[]{:S(2)}) collective-permute-start(f32[32,1,16,128]{3,0,2,1:T(8,128)S(1)} %get-tuple-element.30), channel_id=1, source_target_pairs={{0,4},{4,8},{8,12},{12,16},{16,20},{20,24},{24,28},{1,5},{5,9},{9,... | collective-permute-start | bytes 786440 | tf_op jit(solution)/shard_map/ppermute | solution.py:26
  122.1 6.2 %collective-permute-start.11 = (f32[32,6,1,128]{3,0,2,1:T(8,128)S(1)}, f32[32,6,1,128]{3,0,2,1:T(8,128)S(1)}, u32[]{:S(2)}, u32[]{:S(2)}) collective-permute-start(f32[32,6,1,128]{3,0,2,1:T(8,128)S(1)} %get-tuple-element.23), channel_id=1, source_target_pairs={{0,1},{1,2},{2,3},{4,5},{5,6},{6,7},{8,9},{9,10},{10,11},{12,13},{... | collective-permute-start | bytes 294920 | tf_op jit(solution)/shard_map/ppermute | solution.py:26
  124.0 5.9 %collective-permute-start.10 = (f32[32,6,1,128]{3,0,2,1:T(8,128)S(1)}, f32[32,6,1,128]{3,0,2,1:T(8,128)S(1)}, u32[]{:S(2)}, u32[]{:S(2)}) collective-permute-start(f32[32,6,1,128]{3,0,2,1:T(8,128)S(1)} %get-tuple-element.22), channel_id=1, source_target_pairs={{1,0},{2,1},{3,2},{5,4},{6,5},{7,6},{9,8},{10,9},{11,10},{13,12},{... | collective-permute-start | bytes 294920 | tf_op jit(solution)/shard_map/ppermute | solution.py:28
  131.0 8.4 %collective-permute-start.12 = (f32[32,1,16,128]{3,0,2,1:T(8,128)S(1)}, f32[32,1,16,128]{3,0,2,1:T(8,128)S(1)}, u32[]{:S(2)}, u32[]{:S(2)}) collective-permute-start(f32[32,1,16,128]{3,0,2,1:T(8,128)S(1)} %get-tuple-element.29), channel_id=1, source_target_pairs={{4,0},{8,4},{12,8},{16,12},{20,16},{24,20},{28,24},{5,1},{9,5},{13... | collective-permute-start | bytes 786440 | tf_op jit(solution)/shard_map/ppermute | solution.py:28
  132.3 13.6 %collective-permute-start.13 = (f32[32,1,16,128]{3,0,2,1:T(8,128)S(1)}, f32[32,1,16,128]{3,0,2,1:T(8,128)S(1)}, u32[]{:S(2)}, u32[]{:S(2)}) collective-permute-start(f32[32,1,16,128]{3,0,2,1:T(8,128)S(1)} %get-tuple-element.28), channel_id=1, source_target_pairs={{0,4},{4,8},{8,12},{12,16},{16,20},{20,24},{24,28},{1,5},{5,9},{9,... | collective-permute-start | bytes 786440 | tf_op jit(solution)/shard_map/ppermute | solution.py:26
  145.8 6.5 %collective-permute-start.15 = (f32[32,6,1,128]{3,0,2,1:T(8,128)S(1)}, f32[32,6,1,128]{3,0,2,1:T(8,128)S(1)}, u32[]{:S(2)}, u32[]{:S(2)}) collective-permute-start(f32[32,6,1,128]{3,0,2,1:T(8,128)S(1)} %get-tuple-element.21), channel_id=1, source_target_pairs={{0,1},{1,2},{2,3},{4,5},{5,6},{6,7},{8,9},{9,10},{10,11},{12,13},{... | collective-permute-start | bytes 294920 | tf_op jit(solution)/shard_map/ppermute | solution.py:26
  147.8 5.9 %collective-permute-start.14 = (f32[32,6,1,128]{3,0,2,1:T(8,128)S(1)}, f32[32,6,1,128]{3,0,2,1:T(8,128)S(1)}, u32[]{:S(2)}, u32[]{:S(2)}) collective-permute-start(f32[32,6,1,128]{3,0,2,1:T(8,128)S(1)} %get-tuple-element.20), channel_id=1, source_target_pairs={{1,0},{2,1},{3,2},{5,4},{6,5},{7,6},{9,8},{10,9},{11,10},{13,12},{... | collective-permute-start | bytes 294920 | tf_op jit(solution)/shard_map/ppermute | solution.py:28
  (5 other events, 48.3 us)
where the time goes:
time: 158 us; the launch traced here: 156 us
  starting transfers between devices  65.8 us (42%)
  local copies, waits for them, and re-layouts  35.1 us (22%)
  waiting for transfers between devices  32.8 us (21%)
  other arithmetic  11 us (7%)
  matrix products  10.2 us (6%)
    ppermute x10, starting transfers between devices, padded_2(): lax.ppermute(tail, axis, [(i, (i + 1) % count) for i in range(ends)])  34.1 us
    ppermute x10, starting transfers between devices, padded_2(): lax.ppermute(head, axis, [((i + 1) % count, i) for i in range(ends)])  19.7 us
    ppermute x10, waiting for transfers between devices, padded_2(): lax.ppermute(tail, axis, [(i, (i + 1) % count) for i in range(ends)])  19.3 us
    ppermute x4, starting transfers between devices, shifted(): return lax.ppermute(block, axis, route)  12 us
    ppermute x10, waiting for transfers between devices, padded_2(): lax.ppermute(head, axis, [((i + 1) % count, i) for i in range(ends)])  10.5 us
    mul x3, local copies, waits for them, and re-layouts, advance(): time_step * source  10.3 us
    unnamed x43, local copies, waits for them, and re-layouts  9.05 us
    dot_general x4, matrix products, advance(): jnp.dot(mixing, center.reshape(species, -1), precision=lax.Precision.HIGH...  8.08 us
  transfers between devices with their start and end apart: 24, of which 11 were waited for; matrix products, arithmetic and copies ran while one was open for 31% of the time, Pallas kernels for 0%

commit v1 on v0

v1 whole, which is shorter than its diff:
```python
import jax
import jax.numpy as jnp
from jax import lax
from jax.experimental import pallas as pl
from jax.experimental.pallas import tpu as pltpu
from jax.sharding import PartitionSpec as P

BIN_XY = 4
BIN_Z = 8
SLOTS = 16
SUBSTEPS = 4
CHUNK = 8
GROUPS = 9

time_step = 0.15
move_step = 0.1
spread_sq = 8.0
shifts = ((-1, -1), (-1, 0), (-1, 1), (0, -1), (0, 1), (1, -1), (1, 0), (1, 1))
MESH = pl.DeviceIdType.MESH


def split(value):
    high = value.astype(jnp.bfloat16)
    return high, (value - high.astype(jnp.float32)).astype(jnp.bfloat16)


def kernel(
    field_ref, rates_ref, mixing_ref, sec_ref, pos_ref, stiff_ref, occ_ref, off_ref, state_ref, live_ref,
    out_ref, disp_ref, arrived_ref,
    buf, halo_x, halo_y, src, pts, nb, own, acc, payload,
    sx, rx, sy, ry, sp, rp, sm, rm, local,
):
    nx, ny, species, nz = buf.shape[1:]
    bins_y, lanes = stiff_ref.shape[1:]
    halves = ny // CHUNK
    gx, gy = lax.axis_index("gx"), lax.axis_index("gy")
    n_gx, n_gy = lax.axis_size("gx"), lax.axis_size("gy")

    def exists(dx, dy):
        ok = None
        for coord, count, delta in ((gx, n_gx, dx), (gy, n_gy, dy)):
            if delta != 0:
                one = coord > 0 if delta < 0 else coord < count - 1
                ok = one if ok is None else jnp.logical_and(ok, one)
        return ok

    def whither(dx, dy):
        return (gx + dx, gy + dy)

    load = pltpu.make_async_copy(field_ref, buf.at[0], local.at[0])
    load.start()

    barrier = pltpu.get_barrier_semaphore()
    for dx, dy in shifts:
        @pl.when(exists(dx, dy))
        def _(dx=dx, dy=dy):
            pl.semaphore_signal(barrier, inc=1, device_id=whither(dx, dy), device_id_type=MESH)

    weight = stiff_ref[0] * occ_ref[0].astype(jnp.float32)
    for by in range(bins_y):
        for plane in range(3):
            pts[1, by + 1, plane : plane + 1, :] = pos_ref[plane, 0, by : by + 1, :]
        pts[1, by + 1, 3:4, :] = weight[by : by + 1]
    for index in range(8):
        payload[index] = state_ref[index] * live_ref[index].astype(jnp.float32)

    across = 1 + (gx > 0).astype(jnp.int32) + (gx < n_gx - 1).astype(jnp.int32)
    along = 1 + (gy > 0).astype(jnp.int32) + (gy < n_gy - 1).astype(jnp.int32)
    pl.semaphore_wait(barrier, across * along - 1)
    load.wait()

    sides = (-1, 1)

    def face_x(t, side, half):
        rows = pl.ds(half * CHUNK, CHUNK)
        return pltpu.make_async_remote_copy(
            src_ref=buf.at[t, 0 if side == 0 else nx - 1, rows],
            dst_ref=halo_x.at[t, 1 - side, rows],
            send_sem=sx.at[t, side, half],
            recv_sem=rx.at[t, side, half],
            device_id=whither(sides[side], 0),
            device_id_type=MESH,
        )

    def face_y(t, side):
        return pltpu.make_async_remote_copy(
            src_ref=buf.at[t, :, 0 if side == 0 else ny - 1],
            dst_ref=halo_y.at[t, 1 - side],
            send_sem=sy.at[t, side],
            recv_sem=ry.at[t, side],
            device_id=whither(0, sides[side]),
            device_id_type=MESH,
        )

    def agents(index):
        dx, dy = shifts[index]
        if dy == 0:
            mine, theirs = pl.ds(1, bins_y), pl.ds(1, bins_y)
        elif dy > 0:
            mine, theirs = pl.ds(bins_y, 1), pl.ds(0, 1)
        else:
            mine, theirs = pl.ds(1, 1), pl.ds(bins_y + 1, 1)
        return pltpu.make_async_remote_copy(
            src_ref=pts.at[1, mine],
            dst_ref=pts.at[1 - dx, theirs],
            send_sem=sp.at[index],
            recv_sem=rp.at[index],
            device_id=whither(dx, dy),
            device_id_type=MESH,
        )

    def migrants(index):
        dx, dy = shifts[index]
        return pltpu.make_async_remote_copy(
            src_ref=payload.at[index],
            dst_ref=arrived_ref.at[index],
            send_sem=sm.at[index],
            recv_sem=rm.at[index],
            device_id=whither(dx, dy),
            device_id_type=MESH,
        )

    def send(copy, dx, dy):
        @pl.when(exists(dx, dy))
        def _():
            copy.start()

    def landed(copy, dx, dy):
        @pl.when(exists(-dx, -dy))
        def _():
            copy.wait_recv()

    for half in range(halves):
        for side in range(2):
            send(face_x(0, side, half), sides[side], 0)
        if half == 0:
            for side in range(2):
                send(face_y(0, side), 0, sides[side])
    for index in range(8):
        send(agents(index), *shifts[index])
    for index in range(8):
        send(migrants(index), *shifts[index])

    for side in range(2):
        @pl.when(jnp.logical_not(exists(sides[side], 0)))
        def _(side=side):
            def fill(row, carry):
                for t in range(SUBSTEPS):
                    halo_x[t, side, row] = jnp.zeros((species, nz), jnp.float32)
                return carry
            lax.fori_loop(0, ny, fill, 0)

        @pl.when(jnp.logical_not(exists(0, sides[side])))
        def _(side=side):
            for t in range(SUBSTEPS):
                halo_y[t, side] = jnp.zeros((nx, species, nz), jnp.float32)

    for index in range(8):
        dx, dy = shifts[index]

        @pl.when(jnp.logical_not(exists(-dx, -dy)))
        def _(index=index, dx=dx, dy=dy):
            arrived_ref[index] = jnp.zeros(arrived_ref.shape[1:], jnp.float32)
            rows = pl.ds(1, bins_y) if dy == 0 else pl.ds(0 if dy > 0 else bins_y + 1, 1)
            count = bins_y if dy == 0 else 1
            pts[1 - dx, rows] = jnp.zeros((count,) + pts.shape[2:], jnp.float32)

    depth = lax.broadcasted_iota(jnp.int32, (nz, lanes), 0)
    layer = lax.broadcasted_iota(jnp.int32, (1, lanes), 1) // SLOTS
    for by in range(bins_y):
        place = off_ref[0, by : by + 1, :]
        alive = occ_ref[0, by : by + 1, :].astype(jnp.float32) * time_step
        secreted = jnp.concatenate(split(sec_ref[:, 0, by, :] * alive), axis=0)
        cell = jnp.where(depth == layer * BIN_Z + (place & (BIN_Z - 1)), place >> 3, -1)

        def deposit(ox, carry, by=by, secreted=secreted, cell=cell):
            hits = jnp.concatenate(
                [
                    jnp.where(cell == ox * BIN_XY + oy, 1.0, 0.0).astype(jnp.bfloat16)
                    for oy in range(BIN_XY)
                ],
                axis=0,
            )
            total = lax.dot_general(
                secreted, hits, (((1,), (1,)), ((), ())), preferred_element_type=jnp.float32
            )
            total = total[:species] + total[species:]
            for oy in range(BIN_XY):
                src[ox, by * BIN_XY + oy] = total[:, oy * nz : (oy + 1) * nz]
            return carry

        lax.fori_loop(0, BIN_XY, deposit, 0)

    mix_high, mix_low = split(mixing_ref[...] * time_step)
    mix = jnp.concatenate([mix_high, mix_high, mix_low], axis=1)
    reach = rates_ref[...] * time_step
    keep = 1.0 - 6.0 * reach
    reach = jnp.broadcast_to(reach, (species, nz))
    keep = jnp.broadcast_to(keep, (species, nz))
    column = lax.broadcasted_iota(jnp.int32, (species, nz), 1)

    def block(t, x, half):
        first = half * CHUNK
        cells = jnp.concatenate([buf[t, x, first + k] for k in range(CHUNK)], axis=1)
        high, low = split(cells)
        mixed = jnp.dot(
            mix, jnp.concatenate([high, low, high], axis=0), preferred_element_type=jnp.float32
        )
        for k in range(CHUNK):
            y = first + k
            here = buf[t, x, y]
            beside = halo_x[t, 0, y] if x == 0 else buf[t, x - 1, y]
            beside = beside + (halo_x[t, 1, y] if x == nx - 1 else buf[t, x + 1, y])
            beside = beside + (halo_y[t, 0, x] if y == 0 else buf[t, x, y - 1])
            beside = beside + (halo_y[t, 1, x] if y == ny - 1 else buf[t, x, y + 1])
            beside = beside + jnp.where(column == 0, 0.0, pltpu.roll(here, 1, 1))
            beside = beside + jnp.where(column == nz - 1, 0.0, pltpu.roll(here, nz - 1, 1))
            buf[t + 1, x, y] = (
                keep * here + reach * beside + mixed[:, k * nz : (k + 1) * nz] + src[x, y]
            )

    def gather_agents():
        for index in range(8):
            landed(agents(index), *shifts[index])
        for group in range(GROUPS):
            dx, dy = group // 3, group % 3
            for by in range(bins_y):
                row = group * bins_y + by
                for plane in range(4):
                    nb[plane, row : row + 1, :] = pts[dx, by + dy, plane : plane + 1, :]
                for plane in range(3):
                    own[plane, row : row + 1, :] = pts[1, by + 1, plane : plane + 1, :]
        used = GROUPS * bins_y
        if nb.shape[1] > used:
            for plane in range(4):
                nb[plane, used:, :] = jnp.zeros((nb.shape[1] - used, lanes), jnp.float32)
            for plane in range(3):
                own[plane, used:, :] = jnp.zeros((nb.shape[1] - used, lanes), jnp.float32)
        acc[...] = jnp.zeros(acc.shape, jnp.float32)

    slot = lax.broadcasted_iota(jnp.int32, (1, lanes), 1)
    span = 2 * SLOTS - 1
    share = -(-(2 * span + 1) // (SUBSTEPS - 1))

    def forces(t):
        def pairs(k, carry):
            d = (t - 1) * share + k - span
            other = slot + d
            near = jnp.abs((other >> 4) - (slot >> 4)) <= 1
            near = jnp.logical_and(near, jnp.logical_and(other >= 0, other < lanes))
            turn = lax.rem(lanes - d, lanes)
            apart = [own[plane] - pltpu.roll(nb[plane], turn, 1) for plane in range(3)]
            heavy = jnp.where(near, pltpu.roll(nb[3], turn, 1), 0.0)
            square = apart[0] * apart[0] + apart[1] * apart[1] + apart[2] * apart[2]
            strength = heavy * jnp.exp(square * (-1.0 / spread_sq))
            for plane in range(3):
                acc[plane] += apart[plane] * strength
            return carry

        lax.fori_loop(0, share, pairs, 0)

    def substep(t, carry):
        for side in range(2):
            landed(face_y(t, side), 0, sides[side])
        for half in range(halves):
            for side in (1, 0):
                landed(face_x(t, side, half), sides[side], 0)
                mine = 1 - side
                block(t, 0 if mine == 0 else nx - 1, half)

                @pl.when(t < SUBSTEPS - 1)
                def _(mine=mine, half=half):
                    send(face_x(t + 1, mine, half), sides[mine], 0)

            if half == 0:
                for x in range(1, nx - 1):
                    for part in range(halves):
                        block(t, x, part)

                @pl.when(t == 1)
                def _():
                    gather_agents()

                @pl.when(t >= 1)
                def _():
                    forces(t)

        @pl.when(t < SUBSTEPS - 1)
        def _():
            for side in range(2):
                send(face_y(t + 1, side), 0, sides[side])

        return carry

    lax.fori_loop(0, SUBSTEPS, substep, 0)

    store = pltpu.make_async_copy(buf.at[SUBSTEPS], out_ref, local.at[0])
    store.start()
    scale = move_step * occ_ref[0].astype(jnp.float32)
    for plane in range(3):
        force = acc[plane, 0:bins_y, :]
        for group in range(1, GROUPS):
            force = force + acc[plane, group * bins_y : (group + 1) * bins_y, :]
        disp_ref[plane, 0] = scale * force

    for index in range(8):
        landed(migrants(index), *shifts[index])

    def sent(copy, dx, dy):
        @pl.when(exists(dx, dy))
        def _():
            copy.wait_send()

    for index in range(8):
        sent(agents(index), *shifts[index])
        sent(migrants(index), *shifts[index])

    def drain(t, carry):
        for side in range(2):
            for half in range(halves):
                sent(face_x(t, side, half), sides[side], 0)
            sent(face_y(t, side), 0, sides[side])
        return carry

    lax.fori_loop(0, SUBSTEPS, drain, 0)
    store.wait()


def on_device(
    field, rates, mixing, secretion, positions, stiffness, occupancy, offsets, migrant_state, migrant_live
):
    species, nx, ny, nz = field.shape
    bins_y, lanes = stiffness.shape[1:]
    halves = ny // CHUNK
    kinds, state, slots = migrant_state.shape
    rows = -(-GROUPS * bins_y // 8) * 8
    cells = jnp.transpose(field, (1, 2, 0, 3))
    vmem = pl.BlockSpec(memory_space=pltpu.VMEM)
    anywhere = pl.BlockSpec(memory_space=pl.ANY)
    dma = pltpu.SemaphoreType.DMA
    result, moved, arrived = pl.pallas_call(
        kernel,
        out_shape=(
            jax.ShapeDtypeStruct(cells.shape, jnp.float32),
            jax.ShapeDtypeStruct(positions.shape, jnp.float32),
            jax.ShapeDtypeStruct(migrant_state.shape, jnp.float32),
        ),
        in_specs=[anywhere] + [vmem] * 9,
        out_specs=(anywhere, vmem, vmem),
        scratch_shapes=[
            pltpu.VMEM((SUBSTEPS + 1, nx, ny, species, nz), jnp.float32),
            pltpu.VMEM((SUBSTEPS, 2, ny, species, nz), jnp.float32),
            pltpu.VMEM((SUBSTEPS, 2, nx, species, nz), jnp.float32),
            pltpu.VMEM((nx, ny, species, nz), jnp.float32),
            pltpu.VMEM((3, bins_y + 2, 8, lanes), jnp.float32),
            pltpu.VMEM((4, rows, lanes), jnp.float32),
            pltpu.VMEM((3, rows, lanes), jnp.float32),
            pltpu.VMEM((3, rows, lanes), jnp.float32),
            pltpu.VMEM(migrant_state.shape, jnp.float32),
            dma((SUBSTEPS, 2, halves)),
            dma((SUBSTEPS, 2, halves)),
            dma((SUBSTEPS, 2)),
            dma((SUBSTEPS, 2)),
            dma((8,)),
            dma((8,)),
            dma((8,)),
            dma((8,)),
            dma((1,)),
        ],
        compiler_params=pltpu.CompilerParams(
            collective_id=0, has_side_effects=True, vmem_limit_bytes=40 * 1024 * 1024
        ),
        name="tumour_step",
    )(
        cells,
        rates[:, None],
        mixing,
        secretion,
        positions,
        stiffness,
        occupancy,
        offsets,
        migrant_state,
        migrant_live,
    )
    return jnp.transpose(result, (2, 0, 1, 3)), moved, arrived


def solution(mesh):
    return jax.shard_map(
        on_device,
        mesh=mesh,
        in_specs=(
            P(None, "gx", "gy", None),
            P(),
            P(),
            P(None, "gx", "gy", None),
            P(None, "gx", "gy", None),
            P("gx", "gy", None),
            P("gx", "gy", None),
            P("gx", "gy", None),
            P(None, "gx", "gy"),
            P(None, "gx", "gy"),
        ),
        out_specs=(P(None, "gx", "gy", None), P(None, "gx", "gy", None), P(None, "gx", "gy")),
        check_vma=False,
    )
```

time: 158 us -> 64.6 us (0.41)
  the two profiles are of different devices: /device:TPU:1 before, /device:TPU:9 now
where the time goes in v1:
time: 64.6 us; the launch traced here: 64.4 us
  Pallas kernels  57.2 us (89%)
  local copies, waits for them, and re-layouts  6.49 us (10%)
  between operations  0.76 us (1%)
    pallas_call x1, Pallas kernels, on_device(): pl.pallas_call(kernel, out_shape=(jax.ShapeDtypeStruct(cells.shape, jnp.f...  57.2 us
    unnamed x21, local copies, waits for them, and re-layouts  6.41 us

profile of v1, /device:TPU:9, one launch (start us, length us, event | category | flops | bytes accessed | tf_op | source)
XLA Modules:
  0.0 64.4 jit_solution(3373868406148066383)
XLA Ops:
  0.6 0.0 copy-start.7
  0.6 0.6 %copy-done.7 = f32[32]{0:T(128)S(1)} copy-done((f32[32]{0:T(128)S(1)}, f32[32]{0:T(128)}, u32[]{:S(2)}) %copy-start.7) | copy-done | bytes 152
  1.3 0.1 copy.14.rates_ref
  1.4 0.9 %copy.15.state_ref = f32[8,35,128]{2,1,0:T(8,128)S(1)} copy(f32[8,35,128]{2,0,1:T(8,128)} %param.18) | data formatting | bytes 286720 | tf_op args[8]
  2.3 0.0 copy-start
  2.3 0.0 copy-start.1
  2.3 0.0 copy-start.2
  2.4 0.0 copy-start.3
  2.4 0.0 copy-start.4
  2.4 0.0 copy-start.5
  2.4 0.0 copy-start.6
  2.4 1.9 %copy.19 = f32[32,4,16,128]{3,0,2,1:T(8,128)S(1)} copy(f32[32,4,16,128]{3,2,1,0:T(8,128)} %param.10) | data formatting | bytes 2097152 | tf_op args[0]
  4.3 0.0 copy-done
  4.3 0.0 copy-done.1
  4.3 0.0 copy-done.2
  4.3 0.0 copy-done.3
  4.3 0.0 copy-done.4
  4.4 0.0 copy-done.5
  4.4 0.0 copy-done.6
  4.4 57.2 %tumour_step.1 = (f32[4,16,32,128]{3,2,1,0:T(8,128)S(1)}, f32[3,1,4,256]{3,2,1,0:T(4,128)S(1)}, f32[8,35,128]{2,1,0:T(8,128)S(1)}) custom-call(f32[4,16,32,128]{3,2,1,0:T(8,128)S(1)} %bitcast.5, f32[32,1]{1,0:T(8,128)S(1)} %copy.14.rates_ref, f32[32,32]{1,0:T(8,128)S(1)} %copy-done.1, f32[32,1,4,256]{3,2,1,0:T(4,128)S(1)} %copy-done, ...), custom_call_target="tpu_custom_call" | custom-call | tf_op jit(solution)/shard_map/tumour_step/pallas_call | solution.py:341
  61.6 1.6 %copy.16 = f32[32,4,16,128]{3,2,1,0:T(8,128)} copy(f32[32,4,16,128]{3,0,2,1:T(8,128)S(1)} %bitcast.6) | data formatting | bytes 2097152
  63.2 0.7 %copy.17 = f32[8,35,128]{2,0,1:T(8,128)} copy(f32[8,35,128]{2,1,0:T(8,128)S(1)} %get-tuple-element.11) | data formatting | bytes 286720
  63.8 0.6 copy.21
Async XLA Ops:
  0.6 0.7 %copy-start.7 = (f32[32]{0:T(128)S(1)}, f32[32]{0:T(128)}, u32[]{:S(2)}) copy-start(f32[32]{0:T(128)} %param.11) | copy-start | bytes 388
  2.3 2.0 %copy-start = (f32[32,1,4,256]{3,2,1,0:T(4,128)S(1)}, f32[32,1,4,256]{3,2,1,0:T(4,128)}, u32[]{:S(2)}) copy-start(f32[32,1,4,256]{3,2,1,0:T(4,128)} %sec_ref.1) | copy-start | bytes 393220
  2.3 2.0 %copy-start.1 = (f32[32,32]{1,0:T(8,128)S(1)}, f32[32,32]{1,0:T(8,128)}, u32[]{:S(2)}) copy-start(f32[32,32]{1,0:T(8,128)} %mixing_ref.1) | copy-start | bytes 12292
  2.3 2.0 %copy-start.2 = (f32[3,1,4,256]{3,2,1,0:T(4,128)S(1)}, f32[3,1,4,256]{3,2,1,0:T(4,128)}, u32[]{:S(2)}) copy-start(f32[3,1,4,256]{3,2,1,0:T(4,128)} %pos_ref.1) | copy-start | bytes 36868
  2.4 2.0 %copy-start.3 = (f32[1,4,256]{2,1,0:T(4,128)S(1)}, f32[1,4,256]{2,1,0:T(4,128)}, u32[]{:S(2)}) copy-start(f32[1,4,256]{2,1,0:T(4,128)} %stiff_ref.1) | copy-start | bytes 12292
  2.4 2.0 %copy-start.4 = (s32[1,4,256]{2,1,0:T(4,128)S(1)}, s32[1,4,256]{2,1,0:T(4,128)}, u32[]{:S(2)}) copy-start(s32[1,4,256]{2,1,0:T(4,128)} %occ_ref.1) | copy-start | bytes 12292
  2.4 2.0 %copy-start.5 = (s32[1,4,256]{2,1,0:T(4,128)S(1)}, s32[1,4,256]{2,1,0:T(4,128)}, u32[]{:S(2)}) copy-start(s32[1,4,256]{2,1,0:T(4,128)} %off_ref.1) | copy-start | bytes 12292
  2.4 2.0 %copy-start.6 = (s32[8,1,128]{2,1,0:T(1,128)S(1)}, s32[8,1,128]{2,1,0:T(1,128)}, u32[]{:S(2)}) copy-start(s32[8,1,128]{2,1,0:T(1,128)} %live_ref.1) | copy-start | bytes 12292

commit v2 on v1

v2 whole, which is shorter than its diff:
```python
import jax
import jax.numpy as jnp
from jax import lax
from jax.experimental import pallas as pl
from jax.experimental.pallas import tpu as pltpu
from jax.sharding import PartitionSpec as P

BIN_XY = 4
BIN_Z = 8
SLOTS = 16
SUBSTEPS = 4
CHUNK = 8
GROUPS = 9

time_step = 0.15
move_step = 0.1
spread_sq = 8.0
shifts = ((-1, -1), (-1, 0), (-1, 1), (0, -1), (0, 1), (1, -1), (1, 0), (1, 1))
MESH = pl.DeviceIdType.MESH


def split(value):
    high = value.astype(jnp.bfloat16)
    return high, (value - high.astype(jnp.float32)).astype(jnp.bfloat16)


def kernel(
    field_ref, rates_ref, mixing_ref, sec_ref, pos_ref, stiff_ref, occ_ref, off_ref, state_ref, live_ref,
    out_ref, disp_ref, arrived_ref,
    home, buf, swap_to, swap_from, face_to, face_from, edge_from, ends_to, ends_from,
    sec_to, sec_from, off_from, src, pts, nb, own, acc, payload, landing,
    s_swap, r_swap, s_face, r_face, s_edge, r_edge, s_ends, r_ends, s_sec, r_sec,
    s_pts, r_pts, s_mig, r_mig, local, stored,
):
    nx, ny, species, nz = home.shape
    bins_y, lanes = stiff_ref.shape[1:]
    halves = ny // CHUNK
    pairs = CHUNK // 2
    mid = nz // 2
    groups = ((0, nx - 1), tuple(range(1, nx - 1)))
    gx, gy = lax.axis_index("gx"), lax.axis_index("gy")
    n_gx, n_gy = lax.axis_size("gx"), lax.axis_size("gy")
    p = lax.rem(gx, 2)
    mate = (gx + 1 - 2 * p, gy)
    sides = (-1, 1)

    def exists(dx, dy):
        ok = None
        for coord, count, delta in ((gx, n_gx, dx), (gy, n_gy, dy)):
            if delta != 0:
                one = coord >= -delta if delta < 0 else coord < count - delta
                ok = one if ok is None else jnp.logical_and(ok, one)
        return ok

    load = pltpu.make_async_copy(field_ref, home, local.at[0])
    load.start()

    barrier = pltpu.get_barrier_semaphore()
    for dx, dy in shifts + ((-2, 0), (2, 0)):
        @pl.when(exists(dx, dy))
        def _(dx=dx, dy=dy):
            pl.semaphore_signal(barrier, inc=1, device_id=(gx + dx, gy + dy), device_id_type=MESH)

    alive = occ_ref[0].astype(jnp.float32)
    weight = stiff_ref[0] * alive
    for by in range(bins_y):
        for plane in range(3):
            pts[1, by + 1, plane : plane + 1, :] = pos_ref[plane, 0, by : by + 1, :]
        pts[1, by + 1, 3:4, :] = weight[by : by + 1]
        sec_to[by] = sec_ref[:, 0, by, :] * (alive[by : by + 1] * time_step)

    column = lax.broadcasted_iota(jnp.int32, (species, nz), 1)
    kept = (column // mid) == p
    low = column < mid
    inner = column & (mid - 1)
    rim = (1 - p) * (mid - 1)

    def turned(value):
        return pltpu.roll(value, mid, 1)

    def remote(src_ref, dst_ref, send_sem, recv_sem, device):
        return pltpu.make_async_remote_copy(
            src_ref=src_ref,
            dst_ref=dst_ref,
            send_sem=send_sem,
            recv_sem=recv_sem,
            device_id=device,
            device_id_type=MESH,
        )

    def swap(way, x, half):
        rows = pl.ds(half * pairs, pairs)
        return remote(
            swap_to.at[way, x, rows], swap_from.at[way, x, rows],
            s_swap.at[way, x, half], r_swap.at[way, x, half], mate,
        )

    def face(t, side, half):
        rows = pl.ds(half * pairs, pairs)
        return remote(
            face_to.at[t, side, rows], face_from.at[t, 1 - side, rows],
            s_face.at[t, side, half], r_face.at[t, side, half], (gx + 2 * sides[side], gy),
        )

    def edge(t, side, x):
        return remote(
            buf.at[t, x, 0 if side == 0 else ny - 1], edge_from.at[t, 1 - side, x],
            s_edge.at[t, side, x], r_edge.at[t, side, x], (gx, gy + sides[side]),
        )

    def ends(t, group):
        return remote(
            ends_to.at[t, group], ends_from.at[t, group],
            s_ends.at[t, group], r_ends.at[t, group], mate,
        )

    def secreted():
        width = lanes // 2
        return remote(
            sec_to.at[:, :, pl.ds(pl.multiple_of((1 - p) * width, width), width)],
            sec_from.at[:, :, pl.ds(pl.multiple_of(p * width, width), width)],
            s_sec.at[0], r_sec.at[0], mate,
        )

    def placed():
        return remote(off_ref, off_from, s_sec.at[1], r_sec.at[1], mate)

    def agents(index):
        dx, dy = shifts[index]
        if dy == 0:
            mine, theirs = pl.ds(1, bins_y), pl.ds(1, bins_y)
        elif dy > 0:
            mine, theirs = pl.ds(bins_y, 1), pl.ds(0, 1)
        else:
            mine, theirs = pl.ds(1, 1), pl.ds(bins_y + 1, 1)
        return remote(
            pts.at[1, mine], pts.at[1 - dx, theirs],
            s_pts.at[index], r_pts.at[index], (gx + dx, gy + dy),
        )

    def migrants(index):
        dx, dy = shifts[index]
        return remote(
            payload.at[index], landing.at[index],
            s_mig.at[index], r_mig.at[index], (gx + dx, gy + dy),
        )

    def send(copy, dx, dy):
        @pl.when(exists(dx, dy))
        def _():
            copy.start()

    def landed(copy, dx, dy):
        @pl.when(exists(-dx, -dy))
        def _():
            copy.wait_recv()

    def sent(copy, dx, dy):
        @pl.when(exists(dx, dy))
        def _():
            copy.wait_send()

    def leave(way, x, half, cells):
        for j in range(half * pairs, (half + 1) * pairs):
            swap_to[way, x, j] = jnp.where(kept, turned(cells(2 * j)), cells(2 * j + 1))
        swap(way, x, half).start()

    def enter(way, x, half, cells, keep_in):
        swap(way, x, half).wait_recv()
        for j in range(half * pairs, (half + 1) * pairs):
            came = swap_from[way, x, j]
            keep_in(2 * j, jnp.where(kept, cells(2 * j), came))
            keep_in(2 * j + 1, jnp.where(kept, cells(2 * j + 1), turned(came)))

    across = 1 + (gx > 0).astype(jnp.int32) + (gx < n_gx - 1).astype(jnp.int32)
    along = 1 + (gy > 0).astype(jnp.int32) + (gy < n_gy - 1).astype(jnp.int32)
    beyond = (gx > 1).astype(jnp.int32) + (gx < n_gx - 2).astype(jnp.int32)
    pl.semaphore_wait(barrier, across * along - 1 + beyond)

    secreted().start()
    placed().start()
    load.wait()
    order = [(x, half) for group in groups for half in range(halves) for x in group]
    for x, half in order:
        leave(0, x, half, lambda y, x=x: home[x, y])
    for index in range(8):
        send(agents(index), *shifts[index])
    for index in range(8):
        payload[index] = state_ref[:, index, :] * live_ref[index].astype(jnp.float32)
        send(migrants(index), *shifts[index])

    for side in range(2):
        @pl.when(jnp.logical_not(exists(2 * sides[side], 0)))
        def _(side=side):
            def fill(row, carry):
                for t in range(SUBSTEPS):
                    face_from[t, side, row] = jnp.zeros((species, nz), jnp.float32)
                return carry
            lax.fori_loop(0, ny // 2, fill, 0)

        @pl.when(jnp.logical_not(exists(0, sides[side])))
        def _(side=side):
            for t in range(SUBSTEPS):
                edge_from[t, side] = jnp.zeros((nx, species, nz), jnp.float32)

    for index in range(8):
        dx, dy = shifts[index]

        @pl.when(jnp.logical_not(exists(-dx, -dy)))
        def _(index=index, dx=dx, dy=dy):
            landing[index] = jnp.zeros(landing.shape[1:], jnp.float32)
            rows = pl.ds(1, bins_y) if dy == 0 else pl.ds(0 if dy > 0 else bins_y + 1, 1)
            count = bins_y if dy == 0 else 1
            pts[1 - dx, rows] = jnp.zeros((count,) + pts.shape[2:], jnp.float32)

    secreted().wait_recv()
    placed().wait_recv()
    depth = lax.broadcasted_iota(jnp.int32, (nz, lanes), 0)
    slot = lax.broadcasted_iota(jnp.int32, (1, lanes), 1)
    layer = slot // SLOTS
    ours = (slot // (lanes // 2)) == p
    for by in range(bins_y):
        place = jnp.where(ours, off_ref[0, by : by + 1, :], pltpu.roll(off_from[0, by : by + 1, :], lanes // 2, 1))
        wide = lax.broadcasted_iota(jnp.int32, (species, lanes), 1)
        amount = jnp.where((wide // (lanes // 2)) == p, sec_to[by], sec_from[by])
        amount = jnp.concatenate(split(amount), axis=0)
        cell = jnp.where(depth == layer * BIN_Z + (place & (BIN_Z - 1)), place >> 3, -1)

        def deposit(ox, carry, by=by, amount=amount, cell=cell):
            hits = jnp.concatenate(
                [
                    jnp.where(cell == ox * BIN_XY + oy, 1.0, 0.0).astype(jnp.bfloat16)
                    for oy in range(BIN_XY)
                ],
                axis=0,
            )
            total = lax.dot_general(
                amount, hits, (((1,), (1,)), ((), ())), preferred_element_type=jnp.float32
            )
            total = total[:species] + total[species:]
            for oy in range(BIN_XY):
                src[ox, by * BIN_XY + oy] = total[:, oy * nz : (oy + 1) * nz]
            return carry

        lax.fori_loop(0, BIN_XY, deposit, 0)

    mix_high, mix_low = split(mixing_ref[...] * time_step)
    mix = jnp.concatenate([mix_high, mix_high, mix_low], axis=1)
    diagonal = lax.broadcasted_iota(jnp.int32, (species, species), 0) == lax.broadcasted_iota(
        jnp.int32, (species, species), 1
    )
    reach = jnp.sum(jnp.where(diagonal, rates_ref[...], 0.0), axis=1, keepdims=True) * time_step
    keep = 1.0 - 6.0 * reach
    reach = jnp.broadcast_to(reach, (species, nz))
    keep = jnp.broadcast_to(keep, (species, nz))

    def gather_agents():
        for index in range(8):
            landed(agents(index), *shifts[index])
        for group in range(GROUPS):
            dx, dy = group // 3, group % 3
            for by in range(bins_y):
                row = group * bins_y + by
                for plane in range(4):
                    nb[plane, row : row + 1, :] = pts[dx, by + dy, plane : plane + 1, :]
                for plane in range(3):
                    own[plane, row : row + 1, :] = pts[1, by + 1, plane : plane + 1, :]
        used = GROUPS * bins_y
        if nb.shape[1] > used:
            for plane in range(4):
                nb[plane, used:, :] = jnp.zeros((nb.shape[1] - used, lanes), jnp.float32)
            for plane in range(3):
                own[plane, used:, :] = jnp.zeros((nb.shape[1] - used, lanes), jnp.float32)
        acc[...] = jnp.zeros(acc.shape, jnp.float32)

    span = 2 * SLOTS - 1

    def forces(first, last):
        def pair(d, carry):
            other = slot + d
            near = jnp.abs((other >> 4) - (slot >> 4)) <= 1
            near = jnp.logical_and(near, jnp.logical_and(other >= 0, other < lanes))
            turn = lax.rem(lanes - d, lanes)
            apart = [own[plane] - pltpu.roll(nb[plane], turn, 1) for plane in range(3)]
            heavy = jnp.where(near, pltpu.roll(nb[3], turn, 1), 0.0)
            square = apart[0] * apart[0] + apart[1] * apart[1] + apart[2] * apart[2]
            strength = heavy * jnp.exp(square * (-1.0 / spread_sq))
            for plane in range(3):
                acc[plane] += apart[plane] * strength
            return carry

        lax.fori_loop(first, last, pair, 0)

    def row_of(x, y):
        return (x if x in groups[1] else (1 if x == 0 else 2)) * ny - ny + y

    def show(t, x, half):
        side = 0 if x == 0 else 1
        for j in range(half * pairs, (half + 1) * pairs):
            even, odd = buf[t, x, 2 * j], buf[t, x, 2 * j + 1]
            if side == 0:
                face_to[t, side, j] = jnp.where(low, even, turned(odd))
            else:
                face_to[t, side, j] = jnp.where(low, turned(even), odd)
        send(face(t, side, half), 2 * sides[side], 0)

    def finish(t, group):
        for x in groups[group]:
            for side in range(2):
                send(edge(t, side, x), 0, sides[side])
        packed = jnp.zeros((species, nz), jnp.float32)
        for x in groups[group]:
            for y in range(ny):
                row = row_of(x, y)
                moved = pltpu.roll(buf[t, x, y], lax.rem(row + nz - rim, nz), 1)
                packed = jnp.where(inner == row, moved, packed)
        ends_to[t, group] = packed
        ends(t, group).start()

    def block(t, x, half):
        first = half * CHUNK
        cells = jnp.concatenate([buf[t, x, first + k] for k in range(CHUNK)], axis=1)
        high, less = split(cells)
        mixed = jnp.dot(
            mix, jnp.concatenate([high, less, high], axis=0), preferred_element_type=jnp.float32
        )
        beyond_z = ends_from[t, 0 if x in groups[0] else 1]
        for k in range(CHUNK):
            y = first + k
            here = buf[t, x, y]
            if x > 0:
                beside = buf[t, x - 1, y]
            elif y % 2 == 0:
                beside = jnp.where(low, face_from[t, 0, y // 2], turned(buf[t, nx - 1, y]))
            else:
                beside = turned(jnp.where(low, buf[t, nx - 1, y], face_from[t, 0, y // 2]))
            if x < nx - 1:
                beside = beside + buf[t, x + 1, y]
            elif y % 2 == 0:
                beside = beside + turned(jnp.where(low, face_from[t, 1, y // 2], buf[t, 0, y]))
            else:
                beside = beside + jnp.where(low, turned(buf[t, 0, y]), face_from[t, 1, y // 2])
            beside = beside + (edge_from[t, 0, x] if y == 0 else buf[t, x, y - 1])
            beside = beside + (edge_from[t, 1, x] if y == ny - 1 else buf[t, x, y + 1])
            beside = beside + jnp.where(inner == 0, 0.0, pltpu.roll(here, 1, 1))
            beside = beside + jnp.where(inner == mid - 1, 0.0, pltpu.roll(here, nz - 1, 1))
            arriving = pltpu.roll(beyond_z, lax.rem(rim + nz - row_of(x, y), nz), 1)
            beside = beside + jnp.where(inner == rim, arriving, 0.0)
            buf[t + 1, x, y] = (
                keep * here + reach * beside + mixed[:, k * nz : (k + 1) * nz] + src[x, y]
            )

    def hold(t, x):
        def put(y, value):
            buf[t, x, y] = value
        return put

    gather_agents()
    forces(-span, 0)
    for number, group in enumerate(groups):
        for half in range(halves):
            for x in group:
                enter(0, x, half, lambda y, x=x: home[x, y], hold(0, x))
                if number == 0:
                    show(0, x, half)
        finish(0, number)

    def substep(t, carry):
        for number, group in enumerate(groups):
            for x in group:
                for side in range(2):
                    landed(edge(t, side, x), 0, sides[side])
            ends(t, number).wait_recv()
            for half in range(halves):
                for x in group:
                    if number == 0:
                        side = 1 if x == 0 else 0
                        landed(face(t, side, half), 2 * sides[side], 0)
                    block(t, x, half)

                    @pl.when(t == SUBSTEPS - 1)
                    def _(x=x, half=half):
                        leave(1, x, half, lambda y, x=x: buf[SUBSTEPS, x, y])

                    if number == 0:
                        @pl.when(t < SUBSTEPS - 1)
                        def _(x=x, half=half):
                            show(t + 1, x, half)

            @pl.when(t < SUBSTEPS - 1)
            def _(number=number):
                finish(t + 1, number)

        return carry

    lax.fori_loop(0, SUBSTEPS, substep, 0)

    forces(0, span + 1)
    scale = move_step * alive
    for plane in range(3):
        force = acc[plane, 0:bins_y, :]
        for group in range(1, GROUPS):
            force = force + acc[plane, group * bins_y : (group + 1) * bins_y, :]
        disp_ref[plane, 0] = scale * force

    def store(x, half):
        rows = pl.ds(half * CHUNK, CHUNK)
        return pltpu.make_async_copy(home.at[x, rows], out_ref.at[x, rows], stored.at[x, half])

    for x, half in order:
        def put(y, value, x=x):
            home[x, y] = value

        enter(1, x, half, lambda y, x=x: buf[SUBSTEPS, x, y], put)
        store(x, half).start()

    for index in range(8):
        landed(migrants(index), *shifts[index])
        arrived_ref[:, index, :] = landing[index]
    secreted().wait_send()
    placed().wait_send()
    for index in range(8):
        sent(agents(index), *shifts[index])
        sent(migrants(index), *shifts[index])
    for x, half in order:
        swap(0, x, half).wait_send()
        swap(1, x, half).wait_send()

    def drain(t, carry):
        for side in range(2):
            for half in range(halves):
                sent(face(t, side, half), 2 * sides[side], 0)
            for x in range(nx):
                sent(edge(t, side, x), 0, sides[side])
        for number in range(2):
            ends(t, number).wait_send()
        return carry

    lax.fori_loop(0, SUBSTEPS, drain, 0)
    for x, half in order:
        store(x, half).wait()


def on_device(
    field, rates, mixing, secretion, positions, stiffness, occupancy, offsets, migrant_state, migrant_live
):
    species, nx, ny, nz = field.shape
    bins_y, lanes = stiffness.shape[1:]
    halves = ny // CHUNK
    kinds, state, slots = migrant_state.shape
    rows = -(-GROUPS * bins_y // 8) * 8
    cells = jnp.transpose(field, (1, 2, 0, 3))
    vmem = pl.BlockSpec(memory_space=pltpu.VMEM)
    anywhere = pl.BlockSpec(memory_space=pl.ANY)
    dma = pltpu.SemaphoreType.DMA
    result, moved, arrived = pl.pallas_call(
        kernel,
        out_shape=(
            jax.ShapeDtypeStruct(cells.shape, jnp.float32),
            jax.ShapeDtypeStruct(positions.shape, jnp.float32),
            jax.ShapeDtypeStruct((state, kinds, slots), jnp.float32),
        ),
        in_specs=[anywhere] + [vmem] * 9,
        out_specs=(anywhere, vmem, vmem),
        scratch_shapes=[
            pltpu.VMEM((nx, ny, species, nz), jnp.float32),
            pltpu.VMEM((SUBSTEPS + 1, nx, ny, species, nz), jnp.float32),
            pltpu.VMEM((2, nx, ny // 2, species, nz), jnp.float32),
            pltpu.VMEM((2, nx, ny // 2, species, nz), jnp.float32),
            pltpu.VMEM((SUBSTEPS, 2, ny // 2, species, nz), jnp.float32),
            pltpu.VMEM((SUBSTEPS, 2, ny // 2, species, nz), jnp.float32),
            pltpu.VMEM((SUBSTEPS, 2, nx, species, nz), jnp.float32),
            pltpu.VMEM((SUBSTEPS, 2, species, nz), jnp.float32),
            pltpu.VMEM((SUBSTEPS, 2, species, nz), jnp.float32),
            pltpu.VMEM((bins_y, species, lanes), jnp.float32),
            pltpu.VMEM((bins_y, species, lanes), jnp.float32),
            pltpu.VMEM(offsets.shape, jnp.int32),
            pltpu.VMEM((nx, ny, species, nz), jnp.float32),
            pltpu.VMEM((3, bins_y + 2, 8, lanes), jnp.float32),
            pltpu.VMEM((4, rows, lanes), jnp.float32),
            pltpu.VMEM((3, rows, lanes), jnp.float32),
            pltpu.VMEM((3, rows, lanes), jnp.float32),
            pltpu.VMEM(migrant_state.shape, jnp.float32),
            pltpu.VMEM(migrant_state.shape, jnp.float32),
            dma((2, nx, halves)),
            dma((2, nx, halves)),
            dma((SUBSTEPS, 2, halves)),
            dma((SUBSTEPS, 2, halves)),
            dma((SUBSTEPS, 2, nx)),
            dma((SUBSTEPS, 2, nx)),
            dma((SUBSTEPS, 2)),
            dma((SUBSTEPS, 2)),
            dma((2,)),
            dma((2,)),
            dma((8,)),
            dma((8,)),
            dma((8,)),
            dma((8,)),
            dma((1,)),
            dma((nx, halves)),
        ],
        compiler_params=pltpu.CompilerParams(
            collective_id=0, has_side_effects=True, vmem_limit_bytes=40 * 1024 * 1024
        ),
        name="tumour_step",
    )(
        cells,
        rates[None],
        mixing,
        secretion,
        positions,
        stiffness,
        occupancy,
        offsets,
        jnp.transpose(migrant_state, (1, 0, 2)),
        migrant_live,
    )
    return jnp.transpose(result, (2, 0, 1, 3)), moved, jnp.transpose(arrived, (1, 0, 2))


def solution(mesh):
    return jax.shard_map(
        on_device,
        mesh=mesh,
        in_specs=(
            P(None, "gx", "gy", None),
            P(),
            P(),
            P(None, "gx", "gy", None),
            P(None, "gx", "gy", None),
            P("gx", "gy", None),
            P("gx", "gy", None),
            P("gx", "gy", None),
            P(None, "gx", "gy"),
            P(None, "gx", "gy"),
        ),
        out_specs=(P(None, "gx", "gy", None), P(None, "gx", "gy", None), P(None, "gx", "gy")),
        check_vma=False,
    )
```

time: 64.6 us -> 65.2 us (level)
  the two profiles are of different devices: /device:TPU:9 before, /device:TPU:0 now
where the time goes in v2:
time: 65.2 us; the launch traced here: 65.1 us
  Pallas kernels  58.9 us (90%)
  local copies, waits for them, and re-layouts  5.42 us (8%)
  between operations  0.78 us (1%)
    pallas_call x1, Pallas kernels, on_device(): pl.pallas_call(kernel, out_shape=(jax.ShapeDtypeStruct(cells.shape, jnp.f...  58.9 us
    unnamed x22, local copies, waits for them, and re-layouts  5.42 us

profile of v2, /device:TPU:0, one launch (start us, length us, event | category | flops | bytes accessed | tf_op | source)
XLA Modules:
  0.0 65.1 jit_solution(727339521773303982)
XLA Ops:
  0.6 0.0 copy-start
  0.6 0.0 copy-start.1
  0.7 0.0 copy-start.2
  0.7 0.0 copy-start.3
  0.7 0.0 copy-start.4
  0.7 0.0 copy-start.5
  0.7 0.0 copy-start.6
  0.7 0.0 copy-start.7
  0.7 2.0 %copy.16 = f32[32,4,16,128]{3,0,2,1:T(8,128)S(1)} copy(f32[32,4,16,128]{3,2,1,0:T(8,128)} %param.10) | data formatting | bytes 2097152 | tf_op args[0]
  2.7 0.0 copy-start.8
  2.7 0.0 copy-done
  2.7 0.0 copy-done.1
  2.7 0.0 copy-done.2
  2.7 0.0 copy-done.3
  2.7 0.0 copy-done.4
  2.8 0.0 copy-done.5
  2.8 0.0 copy-done.6
  2.8 0.0 copy-done.7
  2.8 0.6 copy-done.8
  3.4 58.9 %tumour_step.1 = (f32[4,16,32,128]{3,2,1,0:T(8,128)S(1)}, f32[3,1,4,256]{3,2,1,0:T(4,128)S(1)}, f32[35,8,128]{2,1,0:T(8,128)S(1)}) custom-call(f32[4,16,32,128]{3,2,1,0:T(8,128)S(1)} %bitcast.7, f32[1,32]{1,0:T(1,128)S(1)} %bitcast.11, f32[32,32]{1,0:T(8,128)S(1)} %copy-done.2, f32[32,1,4,256]{3,2,1,0:T(4,128)S(1)} %copy-done.1, ...), custom_call_target="tpu_custom_call" | custom-call | tf_op jit(solution)/shard_map/tumour_step/pallas_call | solution.py:456
  62.2 1.6 %copy.14 = f32[32,4,16,128]{3,2,1,0:T(8,128)} copy(f32[32,4,16,128]{3,0,2,1:T(8,128)S(1)} %bitcast.8) | data formatting | bytes 2097152
  63.8 0.6 copy.19
  64.4 0.7 %copy.20 = f32[8,35,128]{2,0,1:T(8,128)} copy(f32[8,35,128]{2,0,1:T(8,128)S(1)} %bitcast.10) | data formatting | bytes 286720
Async XLA Ops:
  0.6 2.1 %copy-start = (f32[8,35,128]{2,0,1:T(8,128)S(1)}, f32[8,35,128]{2,0,1:T(8,128)}, u32[]{:S(2)}) copy-start(f32[8,35,128]{2,0,1:T(8,128)} %param.18) | copy-start | bytes 430084
  0.6 2.1 %copy-start.1 = (f32[32,1,4,256]{3,2,1,0:T(4,128)S(1)}, f32[32,1,4,256]{3,2,1,0:T(4,128)}, u32[]{:S(2)}) copy-start(f32[32,1,4,256]{3,2,1,0:T(4,128)} %sec_ref.1) | copy-start | bytes 393220
  0.7 2.1 %copy-start.2 = (f32[32,32]{1,0:T(8,128)S(1)}, f32[32,32]{1,0:T(8,128)}, u32[]{:S(2)}) copy-start(f32[32,32]{1,0:T(8,128)} %mixing_ref.1) | copy-start | bytes 12292
  0.7 2.1 %copy-start.3 = (f32[3,1,4,256]{3,2,1,0:T(4,128)S(1)}, f32[3,1,4,256]{3,2,1,0:T(4,128)}, u32[]{:S(2)}) copy-start(f32[3,1,4,256]{3,2,1,0:T(4,128)} %pos_ref.1) | copy-start | bytes 36868
  0.7 2.1 %copy-start.4 = (f32[1,4,256]{2,1,0:T(4,128)S(1)}, f32[1,4,256]{2,1,0:T(4,128)}, u32[]{:S(2)}) copy-start(f32[1,4,256]{2,1,0:T(4,128)} %stiff_ref.1) | copy-start | bytes 12292
  0.7 2.1 %copy-start.5 = (s32[1,4,256]{2,1,0:T(4,128)S(1)}, s32[1,4,256]{2,1,0:T(4,128)}, u32[]{:S(2)}) copy-start(s32[1,4,256]{2,1,0:T(4,128)} %occ_ref.1) | copy-start | bytes 12292
  0.7 2.1 %copy-start.6 = (s32[1,4,256]{2,1,0:T(4,128)S(1)}, s32[1,4,256]{2,1,0:T(4,128)}, u32[]{:S(2)}) copy-start(s32[1,4,256]{2,1,0:T(4,128)} %off_ref.1) | copy-start | bytes 12292
  0.7 2.1 %copy-start.7 = (s32[8,1,128]{2,1,0:T(1,128)S(1)}, s32[8,1,128]{2,1,0:T(1,128)}, u32[]{:S(2)}) copy-start(s32[8,1,128]{2,1,0:T(1,128)} %live_ref.1) | copy-start | bytes 12292
  2.7 0.7 %copy-start.8 = (f32[32]{0:T(128)S(1)}, f32[32]{0:T(128)}, u32[]{:S(2)}) copy-start(f32[32]{0:T(128)} %param.11) | copy-start | bytes 388

commit v3 on v2

--- a/solution.py
+++ b/solution.py
@@ -27,12 +27,12 @@
 def kernel(
     field_ref, rates_ref, mixing_ref, sec_ref, pos_ref, stiff_ref, occ_ref, off_ref, state_ref, live_ref,
     out_ref, disp_ref, arrived_ref,
-    home, buf, swap_to, swap_from, face_to, face_from, edge_from, ends_to, ends_from,
+    buf, swap_to, swap_from, face_to, face_from, edge_from, ends_to, ends_from,
     sec_to, sec_from, off_from, src, pts, nb, own, acc, payload, landing,
     s_swap, r_swap, s_face, r_face, s_edge, r_edge, s_ends, r_ends, s_sec, r_sec,
-    s_pts, r_pts, s_mig, r_mig, local, stored,
+    s_pts, r_pts, s_mig, r_mig,
 ):
-    nx, ny, species, nz = home.shape
+    species, nx, ny, nz = field_ref.shape
     bins_y, lanes = stiff_ref.shape[1:]
     halves = ny // CHUNK
     pairs = CHUNK // 2
@@ -52,9 +52,6 @@
                 ok = one if ok is None else jnp.logical_and(ok, one)
         return ok
 
-    load = pltpu.make_async_copy(field_ref, home, local.at[0])
-    load.start()
-
     barrier = pltpu.get_barrier_semaphore()
     for dx, dy in shifts + ((-2, 0), (2, 0)):
         @pl.when(exists(dx, dy))
@@ -179,15 +176,11 @@
 
     secreted().start()
     placed().start()
-    load.wait()
     order = [(x, half) for group in groups for half in range(halves) for x in group]
     for x, half in order:
-        leave(0, x, half, lambda y, x=x: home[x, y])
-    for index in range(8):
-        send(agents(index), *shifts[index])
+        leave(0, x, half, lambda y, x=x: field_ref[:, x, y, :])
     for index in range(8):
         payload[index] = state_ref[:, index, :] * live_ref[index].astype(jnp.float32)
-        send(migrants(index), *shifts[index])
 
     for side in range(2):
         @pl.when(jnp.logical_not(exists(2 * sides[side], 0)))
@@ -355,15 +348,17 @@
             buf[t, x, y] = value
         return put
 
-    gather_agents()
-    forces(-span, 0)
     for number, group in enumerate(groups):
         for half in range(halves):
             for x in group:
-                enter(0, x, half, lambda y, x=x: home[x, y], hold(0, x))
+                enter(0, x, half, lambda y, x=x: field_ref[:, x, y, :], hold(0, x))
                 if number == 0:
                     show(0, x, half)
         finish(0, number)
+    for index in range(8):
+        send(agents(index), *shifts[index])
+    for index in range(8):
+        send(migrants(index), *shifts[index])
 
     def substep(t, carry):
         for number, group in enumerate(groups):
@@ -395,6 +390,8 @@
 
     lax.fori_loop(0, SUBSTEPS, substep, 0)
 
+    gather_agents()
+    forces(-span, 0)
     forces(0, span + 1)
     scale = move_step * alive
     for plane in range(3):
@@ -403,16 +400,11 @@
             force = force + acc[plane, group * bins_y : (group + 1) * bins_y, :]
         disp_ref[plane, 0] = scale * force
 
-    def store(x, half):
-        rows = pl.ds(half * CHUNK, CHUNK)
-        return pltpu.make_async_copy(home.at[x, rows], out_ref.at[x, rows], stored.at[x, half])
-
     for x, half in order:
         def put(y, value, x=x):
-            home[x, y] = value
+            out_ref[:, x, y, :] = value
 
         enter(1, x, half, lambda y, x=x: buf[SUBSTEPS, x, y], put)
-        store(x, half).start()
 
     for index in range(8):
         landed(migrants(index), *shifts[index])
@@ -437,8 +429,6 @@
         return carry
 
     lax.fori_loop(0, SUBSTEPS, drain, 0)
-    for x, half in order:
-        store(x, half).wait()
 
 
 def on_device(
@@ -449,21 +439,18 @@
     halves = ny // CHUNK
     kinds, state, slots = migrant_state.shape
     rows = -(-GROUPS * bins_y // 8) * 8
-    cells = jnp.transpose(field, (1, 2, 0, 3))
     vmem = pl.BlockSpec(memory_space=pltpu.VMEM)
-    anywhere = pl.BlockSpec(memory_space=pl.ANY)
     dma = pltpu.SemaphoreType.DMA
     result, moved, arrived = pl.pallas_call(
         kernel,
         out_shape=(
-            jax.ShapeDtypeStruct(cells.shape, jnp.float32),
+            jax.ShapeDtypeStruct(field.shape, jnp.float32),
             jax.ShapeDtypeStruct(positions.shape, jnp.float32),
             jax.ShapeDtypeStruct((state, kinds, slots), jnp.float32),
         ),
-        in_specs=[anywhere] + [vmem] * 9,
-        out_specs=(anywhere, vmem, vmem),
+        in_specs=[vmem] * 10,
+        out_specs=(vmem, vmem, vmem),
         scratch_shapes=[
-            pltpu.VMEM((nx, ny, species, nz), jnp.float32),
             pltpu.VMEM((SUBSTEPS + 1, nx, ny, species, nz), jnp.float32),
             pltpu.VMEM((2, nx, ny // 2, species, nz), jnp.float32),
             pltpu.VMEM((2, nx, ny // 2, species, nz), jnp.float32),
@@ -496,15 +483,13 @@
             dma((8,)),
             dma((8,)),
             dma((8,)),
-            dma((1,)),
-            dma((nx, halves)),
         ],
         compiler_params=pltpu.CompilerParams(
             collective_id=0, has_side_effects=True, vmem_limit_bytes=40 * 1024 * 1024
         ),
         name="tumour_step",
     )(
-        cells,
+        field,
         rates[None],
         mixing,
         secretion,
@@ -515,7 +500,7 @@
         jnp.transpose(migrant_state, (1, 0, 2)),
         migrant_live,
     )
-    return jnp.transpose(result, (2, 0, 1, 3)), moved, jnp.transpose(arrived, (1, 0, 2))
+    return result, moved, jnp.transpose(arrived, (1, 0, 2))
 
 
 def solution(mesh):

time: 65.2 us -> 59.9 us (0.919)
  Pallas kernels: 58.9 us -> 48.7 us
  local copies, waits for them, and re-layouts: 5.42 us -> 10.1 us
    pallas_call x1, Pallas kernels: 58.9 us -> 48.7 us  [on_device(): pl.pallas_call(kernel, out_shape=(jax.ShapeDtypeStruct(field.shape, jnp.f...]
    unnamed x22 -> x23, local copies, waits for them, and re-layouts: 5.42 us -> 10.1 us
where the time goes in v3:
time: 59.9 us; the launch traced here: 59.4 us
  Pallas kernels  48.7 us (81%)
  local copies, waits for them, and re-layouts  10.1 us (17%)
  between operations  0.66 us (1%)
    pallas_call x1, Pallas kernels, on_device(): pl.pallas_call(kernel, out_shape=(jax.ShapeDtypeStruct(field.shape, jnp.f...  48.7 us
    unnamed x23, local copies, waits for them, and re-layouts  10.1 us

profile of v3, /device:TPU:0, one launch (start us, length us, event | category | flops | bytes accessed | tf_op | source)
XLA Modules:
  0.0 59.4 jit_solution(17124292946941179604)
XLA Ops:
  0.6 0.0 copy-start.9
  0.6 0.6 %copy-done.9 = f32[32]{0:T(128)S(1)} copy-done((f32[32]{0:T(128)S(1)}, f32[32]{0:T(128)}, u32[]{:S(2)}) %copy-start.9) | copy-done | bytes 152
  1.3 0.0 copy-start
  1.3 1.2 %copy-done = f32[32,4,16,128]{3,2,1,0:T(8,128)S(1)} copy-done((f32[32,4,16,128]{3,2,1,0:T(8,128)S(1)}, f32[32,4,16,128]{3,2,1,0:T(8,128)}, u32[]{:S(2)}) %copy-start) | copy-done | bytes 1048600
  2.5 0.0 copy-start.1
  2.5 0.9 %copy-done.1 = f32[8,35,128]{2,0,1:T(8,128)S(1)} copy-done((f32[8,35,128]{2,0,1:T(8,128)S(1)}, f32[8,35,128]{2,0,1:T(8,128)}, u32[]{:S(2)}) %copy-start.1) | copy-done | bytes 143384
  3.4 0.0 copy-start.2
  3.4 0.9 %copy-done.2 = f32[32,1,4,256]{3,2,1,0:T(4,128)S(1)} copy-done((f32[32,1,4,256]{3,2,1,0:T(4,128)S(1)}, f32[32,1,4,256]{3,2,1,0:T(4,128)}, u32[]{:S(2)}) %copy-start.2) | copy-done | bytes 131096
  4.3 0.0 copy-start.3
  4.3 0.7 %copy-done.3 = f32[32,32]{1,0:T(8,128)S(1)} copy-done((f32[32,32]{1,0:T(8,128)S(1)}, f32[32,32]{1,0:T(8,128)}, u32[]{:S(2)}) %copy-start.3) | copy-done | bytes 4120
  5.0 0.0 copy-start.4
  5.0 0.7 %copy-done.4 = f32[3,1,4,256]{3,2,1,0:T(4,128)S(1)} copy-done((f32[3,1,4,256]{3,2,1,0:T(4,128)S(1)}, f32[3,1,4,256]{3,2,1,0:T(4,128)}, u32[]{:S(2)}) %copy-start.4) | copy-done | bytes 12312
  5.8 0.0 copy-start.5
  5.8 0.7 %copy-done.5 = f32[1,4,256]{2,1,0:T(4,128)S(1)} copy-done((f32[1,4,256]{2,1,0:T(4,128)S(1)}, f32[1,4,256]{2,1,0:T(4,128)}, u32[]{:S(2)}) %copy-start.5) | copy-done | bytes 4120
  6.4 0.0 copy-start.6
  6.4 0.7 %copy-done.6 = s32[1,4,256]{2,1,0:T(4,128)S(1)} copy-done((s32[1,4,256]{2,1,0:T(4,128)S(1)}, s32[1,4,256]{2,1,0:T(4,128)}, u32[]{:S(2)}) %copy-start.6) | copy-done | bytes 4120
  7.1 0.0 copy-start.7
  7.1 0.7 %copy-done.7 = s32[1,4,256]{2,1,0:T(4,128)S(1)} copy-done((s32[1,4,256]{2,1,0:T(4,128)S(1)}, s32[1,4,256]{2,1,0:T(4,128)}, u32[]{:S(2)}) %copy-start.7) | copy-done | bytes 4120
  7.8 0.0 copy-start.8
  7.8 0.7 %copy-done.8 = s32[8,1,128]{2,1,0:T(1,128)S(1)} copy-done((s32[8,1,128]{2,1,0:T(1,128)S(1)}, s32[8,1,128]{2,1,0:T(1,128)}, u32[]{:S(2)}) %copy-start.8) | copy-done | bytes 4120
  8.5 48.7 %tumour_step.1 = (f32[32,4,16,128]{3,2,1,0:T(8,128)S(1)}, f32[3,1,4,256]{3,2,1,0:T(4,128)S(1)}, f32[35,8,128]{2,1,0:T(8,128)S(1)}) custom-call(f32[32,4,16,128]{3,2,1,0:T(8,128)S(1)} %copy-done, f32[1,32]{1,0:T(1,128)S(1)} %bitcast.5, f32[32,32]{1,0:T(8,128)S(1)} %copy-done.3, f32[32,1,4,256]{3,2,1,0:T(4,128)S(1)} %copy-done.2, ...), custom_call_target="tpu_custom_call" | custom-call | tf_op jit(solution)/shard_map/tumour_step/pallas_call | solution.py:444
  57.2 1.0 %copy.16 = f32[32,4,16,128]{3,2,1,0:T(8,128)} copy(f32[32,4,16,128]{3,2,1,0:T(8,128)S(1)} %get-tuple-element.12) | data formatting | bytes 2097152
  58.2 0.6 %copy.17 = f32[3,1,4,256]{3,2,1,0:T(4,128)} copy(f32[3,1,4,256]{3,2,1,0:T(4,128)S(1)} %get-tuple-element.13) | data formatting | bytes 24576
  58.8 0.7 %copy.18 = f32[8,35,128]{2,0,1:T(8,128)} copy(f32[8,35,128]{2,0,1:T(8,128)S(1)} %bitcast.4) | data formatting | bytes 286720
Async XLA Ops:
  0.6 0.7 %copy-start.9 = (f32[32]{0:T(128)S(1)}, f32[32]{0:T(128)}, u32[]{:S(2)}) copy-start(f32[32]{0:T(128)} %param.11) | copy-start | bytes 388
  1.3 1.2 %copy-start = (f32[32,4,16,128]{3,2,1,0:T(8,128)S(1)}, f32[32,4,16,128]{3,2,1,0:T(8,128)}, u32[]{:S(2)}) copy-start(f32[32,4,16,128]{3,2,1,0:T(8,128)} %field_ref.1) | copy-start | bytes 3145732
  2.5 0.9 %copy-start.1 = (f32[8,35,128]{2,0,1:T(8,128)S(1)}, f32[8,35,128]{2,0,1:T(8,128)}, u32[]{:S(2)}) copy-start(f32[8,35,128]{2,0,1:T(8,128)} %param.18) | copy-start | bytes 430084
  3.4 0.9 %copy-start.2 = (f32[32,1,4,256]{3,2,1,0:T(4,128)S(1)}, f32[32,1,4,256]{3,2,1,0:T(4,128)}, u32[]{:S(2)}) copy-start(f32[32,1,4,256]{3,2,1,0:T(4,128)} %sec_ref.1) | copy-start | bytes 393220
  4.3 0.7 %copy-start.3 = (f32[32,32]{1,0:T(8,128)S(1)}, f32[32,32]{1,0:T(8,128)}, u32[]{:S(2)}) copy-start(f32[32,32]{1,0:T(8,128)} %mixing_ref.1) | copy-start | bytes 12292
  5.0 0.7 %copy-start.4 = (f32[3,1,4,256]{3,2,1,0:T(4,128)S(1)}, f32[3,1,4,256]{3,2,1,0:T(4,128)}, u32[]{:S(2)}) copy-start(f32[3,1,4,256]{3,2,1,0:T(4,128)} %pos_ref.1) | copy-start | bytes 36868
  5.8 0.7 %copy-start.5 = (f32[1,4,256]{2,1,0:T(4,128)S(1)}, f32[1,4,256]{2,1,0:T(4,128)}, u32[]{:S(2)}) copy-start(f32[1,4,256]{2,1,0:T(4,128)} %stiff_ref.1) | copy-start | bytes 12292
  6.4 0.7 %copy-start.6 = (s32[1,4,256]{2,1,0:T(4,128)S(1)}, s32[1,4,256]{2,1,0:T(4,128)}, u32[]{:S(2)}) copy-start(s32[1,4,256]{2,1,0:T(4,128)} %occ_ref.1) | copy-start | bytes 12292
  7.1 0.7 %copy-start.7 = (s32[1,4,256]{2,1,0:T(4,128)S(1)}, s32[1,4,256]{2,1,0:T(4,128)}, u32[]{:S(2)}) copy-start(s32[1,4,256]{2,1,0:T(4,128)} %off_ref.1) | copy-start | bytes 12292
  7.8 0.7 %copy-start.8 = (s32[8,1,128]{2,1,0:T(1,128)S(1)}, s32[8,1,128]{2,1,0:T(1,128)}, u32[]{:S(2)}) copy-start(s32[8,1,128]{2,1,0:T(1,128)} %live_ref.1) | copy-start | bytes 12292

commit v4 on v3

--- a/solution.py
+++ b/solution.py
@@ -11,6 +11,8 @@
 SUBSTEPS = 4
 CHUNK = 8
 GROUPS = 9
+GRANT = 56 * 1024 * 1024
+PIECES = 4
 
 time_step = 0.15
 move_step = 0.1
@@ -25,8 +27,10 @@
 
 
 def kernel(
+    field_in, rates_in, mixing_in, sec_in, pos_in, stiff_in, occ_in, off_in, state_in, live_in,
+    out_ref, disp_ref, arrived_ref,
     field_ref, rates_ref, mixing_ref, sec_ref, pos_ref, stiff_ref, occ_ref, off_ref, state_ref, live_ref,
-    out_ref, disp_ref, arrived_ref,
+    s_load,
     buf, swap_to, swap_from, face_to, face_from, edge_from, ends_to, ends_from,
     sec_to, sec_from, off_from, src, pts, nb, own, acc, payload, landing,
     s_swap, r_swap, s_face, r_face, s_edge, r_edge, s_ends, r_ends, s_sec, r_sec,
@@ -52,12 +56,34 @@
                 ok = one if ok is None else jnp.logical_and(ok, one)
         return ok
 
+    loads = [
+        pltpu.make_async_copy(there, here, s_load.at[place])
+        for place, (there, here) in enumerate(
+            (
+                (sec_in, sec_ref),
+                (occ_in, occ_ref),
+                (stiff_in, stiff_ref),
+                (pos_in, pos_ref),
+                (off_in, off_ref),
+                (field_in, field_ref),
+                (state_in, state_ref),
+                (live_in, live_ref),
+                (rates_in, rates_ref),
+                (mixing_in, mixing_ref),
+            )
+        )
+    ]
+    for load in loads:
+        load.start()
+
     barrier = pltpu.get_barrier_semaphore()
     for dx, dy in shifts + ((-2, 0), (2, 0)):
         @pl.when(exists(dx, dy))
         def _(dx=dx, dy=dy):
             pl.semaphore_signal(barrier, inc=1, device_id=(gx + dx, gy + dy), device_id_type=MESH)
 
+    for load in loads[:5]:
+        load.wait()
     alive = occ_ref[0].astype(jnp.float32)
     weight = stiff_ref[0] * alive
     for by in range(bins_y):
@@ -176,6 +202,8 @@
 
     secreted().start()
     placed().start()
+    for load in loads[5:]:
+        load.wait()
     order = [(x, half) for group in groups for half in range(halves) for x in group]
     for x, half in order:
         leave(0, x, half, lambda y, x=x: field_ref[:, x, y, :])
@@ -440,6 +468,19 @@
     kinds, state, slots = migrant_state.shape
     rows = -(-GROUPS * bins_y // 8) * 8
     vmem = pl.BlockSpec(memory_space=pltpu.VMEM)
+    hbm = pl.BlockSpec(memory_space=pltpu.HBM)
+    inputs = (
+        field,
+        rates[None],
+        mixing,
+        secretion,
+        positions,
+        stiffness,
+        occupancy,
+        offsets,
+        jnp.transpose(migrant_state, (1, 0, 2)),
+        migrant_live,
+    )
     dma = pltpu.SemaphoreType.DMA
     result, moved, arrived = pl.pallas_call(
         kernel,
@@ -448,9 +489,11 @@
             jax.ShapeDtypeStruct(positions.shape, jnp.float32),
             jax.ShapeDtypeStruct((state, kinds, slots), jnp.float32),
         ),
-        in_specs=[vmem] * 10,
+        in_specs=[hbm] * 10,
         out_specs=(vmem, vmem, vmem),
-        scratch_shapes=[
+        scratch_shapes=[pltpu.VMEM(value.shape, value.dtype) for value in inputs]
+        + [
+            dma((10,)),
             pltpu.VMEM((SUBSTEPS + 1, nx, ny, species, nz), jnp.float32),
             pltpu.VMEM((2, nx, ny // 2, species, nz), jnp.float32),
             pltpu.VMEM((2, nx, ny // 2, species, nz), jnp.float32),
@@ -485,22 +528,38 @@
             dma((8,)),
         ],
         compiler_params=pltpu.CompilerParams(
-            collective_id=0, has_side_effects=True, vmem_limit_bytes=40 * 1024 * 1024
+            collective_id=0, has_side_effects=True, vmem_limit_bytes=GRANT
         ),
         name="tumour_step",
-    )(
-        field,
-        rates[None],
-        mixing,
-        secretion,
-        positions,
-        stiffness,
-        occupancy,
-        offsets,
-        jnp.transpose(migrant_state, (1, 0, 2)),
-        migrant_live,
-    )
+    )(*inputs)
+    results = (result, moved, arrived)
+    result, moved, arrived = pl.pallas_call(
+        deliver,
+        out_shape=tuple(jax.ShapeDtypeStruct(value.shape, value.dtype) for value in results),
+        in_specs=[pl.BlockSpec(memory_space=pl.ANY)] * 3,
+        out_specs=(hbm, hbm, hbm),
+        scratch_shapes=[dma((PIECES + 2,))],
+        compiler_params=pltpu.CompilerParams(vmem_limit_bytes=GRANT),
+        name="deliver",
+    )(*results)
     return result, moved, jnp.transpose(arrived, (1, 0, 2))
+
+
+def deliver(field_ref, disp_ref, arrived_ref, field_out, disp_out, arrived_out, sems):
+    share = field_ref.shape[0] // PIECES
+    routes = [
+        (field_ref.at[pl.ds(piece * share, share)], field_out.at[pl.ds(piece * share, share)])
+        for piece in range(PIECES)
+    ]
+    routes += [(disp_ref, disp_out), (arrived_ref, arrived_out)]
+    copies = [
+        pltpu.make_async_copy(here, there, sems.at[place])
+        for place, (here, there) in enumerate(routes)
+    ]
+    for copy in copies:
+        copy.start()
+    for copy in copies:
+        copy.wait()
 
 
 def solution(mesh):

time: 59.9 us -> 87.9 us (1.47)
  Pallas kernels: 48.7 us -> 87.1 us
  local copies, waits for them, and re-layouts: 10.1 us -> 0 us
    pallas_call x0 -> x1, Pallas kernels: none -> 37.6 us  [on_device(): pl.pallas_call(deliver, out_shape=tuple((jax.ShapeDtypeStruct(value.shape...]
    unnamed x23 -> x0, local copies, waits for them, and re-layouts: 10.1 us -> none
where the time goes in v4:
time: 87.9 us; the launch traced here: 87.8 us
  Pallas kernels  87.1 us (99%)
    pallas_call x1, Pallas kernels, on_device(): pl.pallas_call(kernel, out_shape=(jax.ShapeDtypeStruct(field.shape, jnp.f...  49.5 us
    pallas_call x1, Pallas kernels, on_device(): pl.pallas_call(deliver, out_shape=tuple((jax.ShapeDtypeStruct(value.shape...  37.6 us

profile of v4, /device:TPU:0, one launch (start us, length us, event | category | flops | bytes accessed | tf_op | source)
XLA Modules:
  0.0 87.8 jit_solution(8821537857167414745)
XLA Ops:
  0.6 49.5 %tumour_step.1 = (f32[32,4,16,128]{3,2,1,0:T(8,128)}, f32[3,1,4,256]{3,2,1,0:T(4,128)}, f32[35,8,128]{2,1,0:T(8,128)}) custom-call(f32[32,4,16,128]{3,2,1,0:T(8,128)} %field_in.1, f32[1,32]{1,0:T(1,128)} %bitcast.4, f32[32,32]{1,0:T(8,128)} %mixing_in.1, f32[32,1,4,256]{3,2,1,0:T(4,128)} %sec_in.1, f32[3,1,4,256]{3,2,1,0:T(4,128)} %pos_in.1, ...), custom_call_target="tpu_custom_call" | custom-call | tf_op jit(solution)/shard_map/tumour_step/pallas_call | solution.py:485
  50.2 37.6 %deliver.1 = (f32[32,4,16,128]{3,2,1,0:T(8,128)}, f32[3,1,4,256]{3,2,1,0:T(4,128)}, f32[35,8,128]{2,1,0:T(8,128)}) custom-call(f32[32,4,16,128]{3,2,1,0:T(8,128)} %get-tuple-element.9.field_ref, f32[3,1,4,256]{3,2,1,0:T(4,128)} %get-tuple-element.10.disp_ref, f32[35,8,128]{2,1,0:T(8,128)} %get-tuple-element.11.arrived_ref), custom_call_target="tpu_custom_call" | custom-call | tf_op jit(solution)/shard_map/deliver/pallas_call | solution.py:536

commit v5 on v4

--- a/solution.py
+++ b/solution.py
@@ -428,12 +428,6 @@
             force = force + acc[plane, group * bins_y : (group + 1) * bins_y, :]
         disp_ref[plane, 0] = scale * force
 
-    for x, half in order:
-        def put(y, value, x=x):
-            out_ref[:, x, y, :] = value
-
-        enter(1, x, half, lambda y, x=x: buf[SUBSTEPS, x, y], put)
-
     for index in range(8):
         landed(migrants(index), *shifts[index])
         arrived_ref[:, index, :] = landing[index]
@@ -444,7 +438,6 @@
         sent(migrants(index), *shifts[index])
     for x, half in order:
         swap(0, x, half).wait_send()
-        swap(1, x, half).wait_send()
 
     def drain(t, carry):
         for side in range(2):
@@ -457,6 +450,14 @@
         return carry
 
     lax.fori_loop(0, SUBSTEPS, drain, 0)
+
+    for x, half in order:
+        def put(y, value, x=x):
+            out_ref[:, x, y, :] = value
+
+        enter(1, x, half, lambda y, x=x: buf[SUBSTEPS, x, y], put)
+    for x, half in order:
+        swap(1, x, half).wait_send()
 
 
 def on_device(
@@ -538,27 +539,38 @@
         out_shape=tuple(jax.ShapeDtypeStruct(value.shape, value.dtype) for value in results),
         in_specs=[pl.BlockSpec(memory_space=pl.ANY)] * 3,
         out_specs=(hbm, hbm, hbm),
-        scratch_shapes=[dma((PIECES + 2,))],
+        scratch_shapes=[pltpu.VMEM(value.shape, value.dtype) for value in results]
+        + [dma((PIECES + 2,)), dma((PIECES + 2,))],
         compiler_params=pltpu.CompilerParams(vmem_limit_bytes=GRANT),
         name="deliver",
     )(*results)
     return result, moved, jnp.transpose(arrived, (1, 0, 2))
 
 
-def deliver(field_ref, disp_ref, arrived_ref, field_out, disp_out, arrived_out, sems):
+def deliver(
+    field_ref, disp_ref, arrived_ref, field_out, disp_out, arrived_out,
+    field_held, disp_held, arrived_held, s_in, s_out,
+):
     share = field_ref.shape[0] // PIECES
     routes = [
-        (field_ref.at[pl.ds(piece * share, share)], field_out.at[pl.ds(piece * share, share)])
+        tuple(ref.at[pl.ds(piece * share, share)] for ref in (field_ref, field_held, field_out))
         for piece in range(PIECES)
     ]
-    routes += [(disp_ref, disp_out), (arrived_ref, arrived_out)]
-    copies = [
-        pltpu.make_async_copy(here, there, sems.at[place])
-        for place, (here, there) in enumerate(routes)
+    routes += [(disp_ref, disp_held, disp_out), (arrived_ref, arrived_held, arrived_out)]
+    ins = [
+        pltpu.make_async_copy(here, held, s_in.at[place])
+        for place, (here, held, there) in enumerate(routes)
     ]
-    for copy in copies:
+    outs = [
+        pltpu.make_async_copy(held, there, s_out.at[place])
+        for place, (here, held, there) in enumerate(routes)
+    ]
+    for copy in ins:
         copy.start()
-    for copy in copies:
+    for copy, onward in zip(ins, outs):
+        copy.wait()
+        onward.start()
+    for copy in outs:
         copy.wait()
 
 

time: 87.9 us -> 52.2 us (0.59)
  Pallas kernels: 87.1 us -> 51.4 us
    pallas_call x1, Pallas kernels: 37.6 us -> 2.06 us  [on_device(): pl.pallas_call(deliver, out_shape=tuple((jax.ShapeDtypeStruct(value.shape...]
where the time goes in v5:
time: 52.2 us; the launch traced here: 52 us
  Pallas kernels  51.4 us (98%)
  between operations  0.64 us (1%)
    pallas_call x1, Pallas kernels, on_device(): pl.pallas_call(kernel, out_shape=(jax.ShapeDtypeStruct(field.shape, jnp.f...  49.3 us
    pallas_call x1, Pallas kernels, on_device(): pl.pallas_call(deliver, out_shape=tuple((jax.ShapeDtypeStruct(value.shape...  2.06 us

profile of v5, /device:TPU:0, one launch (start us, length us, event | category | flops | bytes accessed | tf_op | source)
XLA Modules:
  0.0 52.0 jit_solution(14115821166447836985)
XLA Ops:
  0.6 49.3 %tumour_step.1 = (f32[32,4,16,128]{3,2,1,0:T(8,128)}, f32[3,1,4,256]{3,2,1,0:T(4,128)}, f32[35,8,128]{2,1,0:T(8,128)}) custom-call(f32[32,4,16,128]{3,2,1,0:T(8,128)} %field_in.1, f32[1,32]{1,0:T(1,128)} %bitcast.4, f32[32,32]{1,0:T(8,128)} %mixing_in.1, f32[32,1,4,256]{3,2,1,0:T(4,128)} %sec_in.1, f32[3,1,4,256]{3,2,1,0:T(4,128)} %pos_in.1, ...), custom_call_target="tpu_custom_call" | custom-call | tf_op jit(solution)/shard_map/tumour_step/pallas_call | solution.py:486
  49.9 2.1 %deliver.1 = (f32[32,4,16,128]{3,2,1,0:T(8,128)}, f32[3,1,4,256]{3,2,1,0:T(4,128)}, f32[35,8,128]{2,1,0:T(8,128)}) custom-call(f32[32,4,16,128]{3,2,1,0:T(8,128)} %get-tuple-element.9.field_ref, f32[3,1,4,256]{3,2,1,0:T(4,128)} %get-tuple-element.10.disp_ref, f32[35,8,128]{2,1,0:T(8,128)} %get-tuple-element.11.arrived_ref), custom_call_target="tpu_custom_call" | custom-call | tf_op jit(solution)/shard_map/deliver/pallas_call | solution.py:537

commit v6 on v5

--- a/solution.py
+++ b/solution.py
@@ -28,9 +28,10 @@
 
 def kernel(
     field_in, rates_in, mixing_in, sec_in, pos_in, stiff_in, occ_in, off_in, state_in, live_in,
+    field_out, disp_out, arrived_out,
+    field_ref, rates_ref, mixing_ref, sec_ref, pos_ref, stiff_ref, occ_ref, off_ref, state_ref, live_ref,
     out_ref, disp_ref, arrived_ref,
-    field_ref, rates_ref, mixing_ref, sec_ref, pos_ref, stiff_ref, occ_ref, off_ref, state_ref, live_ref,
-    s_load,
+    s_load, s_store, s_block,
     buf, swap_to, swap_from, face_to, face_from, edge_from, ends_to, ends_from,
     sec_to, sec_from, off_from, src, pts, nb, own, acc, payload, landing,
     s_swap, r_swap, s_face, r_face, s_edge, r_edge, s_ends, r_ends, s_sec, r_sec,
@@ -383,10 +384,6 @@
                 if number == 0:
                     show(0, x, half)
         finish(0, number)
-    for index in range(8):
-        send(agents(index), *shifts[index])
-    for index in range(8):
-        send(migrants(index), *shifts[index])
 
     def substep(t, carry):
         for number, group in enumerate(groups):
@@ -414,6 +411,17 @@
             def _(number=number):
                 finish(t + 1, number)
 
+        @pl.when(t == 0)
+        def _():
+            for index in range(8):
+                send(agents(index), *shifts[index])
+
+        for turn in (1, 2):
+            @pl.when(t == turn)
+            def _(turn=turn):
+                for index in range(4 * turn - 4, 4 * turn):
+                    send(migrants(index), *shifts[index])
+
         return carry
 
     lax.fori_loop(0, SUBSTEPS, substep, 0)
@@ -431,6 +439,12 @@
     for index in range(8):
         landed(migrants(index), *shifts[index])
         arrived_ref[:, index, :] = landing[index]
+    stores = [
+        pltpu.make_async_copy(disp_ref, disp_out, s_store.at[0]),
+        pltpu.make_async_copy(arrived_ref, arrived_out, s_store.at[1]),
+    ]
+    for store in stores:
+        store.start()
     secreted().wait_send()
     placed().wait_send()
     for index in range(8):
@@ -456,8 +470,16 @@
             out_ref[:, x, y, :] = value
 
         enter(1, x, half, lambda y, x=x: buf[SUBSTEPS, x, y], put)
+        rows = pl.ds(half * CHUNK, CHUNK)
+        store = pltpu.make_async_copy(
+            out_ref.at[:, x, rows], field_out.at[:, x, rows], s_block.at[x, half]
+        )
+        store.start()
+        stores.append(store)
     for x, half in order:
         swap(1, x, half).wait_send()
+    for store in stores:
+        store.wait()
 
 
 def on_device(
@@ -468,7 +490,6 @@
     halves = ny // CHUNK
     kinds, state, slots = migrant_state.shape
     rows = -(-GROUPS * bins_y // 8) * 8
-    vmem = pl.BlockSpec(memory_space=pltpu.VMEM)
     hbm = pl.BlockSpec(memory_space=pltpu.HBM)
     inputs = (
         field,
@@ -491,10 +512,15 @@
             jax.ShapeDtypeStruct((state, kinds, slots), jnp.float32),
         ),
         in_specs=[hbm] * 10,
-        out_specs=(vmem, vmem, vmem),
+        out_specs=(hbm, hbm, hbm),
         scratch_shapes=[pltpu.VMEM(value.shape, value.dtype) for value in inputs]
         + [
+            pltpu.VMEM(field.shape, jnp.float32),
+            pltpu.VMEM(positions.shape, jnp.float32),
+            pltpu.VMEM((state, kinds, slots), jnp.float32),
             dma((10,)),
+            dma((2,)),
+            dma((nx, halves)),
             pltpu.VMEM((SUBSTEPS + 1, nx, ny, species, nz), jnp.float32),
             pltpu.VMEM((2, nx, ny // 2, species, nz), jnp.float32),
             pltpu.VMEM((2, nx, ny // 2, species, nz), jnp.float32),

time: 52.2 us -> 51 us (0.977)
  Pallas kernels: 51.4 us -> 50.2 us
    pallas_call x1, Pallas kernels: 49.3 us -> 48.2 us  [on_device(): pl.pallas_call(kernel, out_shape=(jax.ShapeDtypeStruct(field.shape, jnp.f...]
where the time goes in v6:
time: 51 us; the launch traced here: 50.9 us
  Pallas kernels  50.2 us (98%)
  between operations  0.64 us (1%)
    pallas_call x1, Pallas kernels, on_device(): pl.pallas_call(kernel, out_shape=(jax.ShapeDtypeStruct(field.shape, jnp.f...  48.2 us
    pallas_call x1, Pallas kernels, on_device(): pl.pallas_call(deliver, out_shape=tuple((jax.ShapeDtypeStruct(value.shape...  2.06 us

profile of v6, /device:TPU:0, one launch (start us, length us, event | category | flops | bytes accessed | tf_op | source)
XLA Modules:
  0.0 50.9 jit_solution(16439798116034991022)
XLA Ops:
  0.6 48.2 %tumour_step.1 = (f32[32,4,16,128]{3,2,1,0:T(8,128)}, f32[3,1,4,256]{3,2,1,0:T(4,128)}, f32[35,8,128]{2,1,0:T(8,128)}) custom-call(f32[32,4,16,128]{3,2,1,0:T(8,128)} %field_in.1, f32[1,32]{1,0:T(1,128)} %bitcast.4, f32[32,32]{1,0:T(8,128)} %mixing_in.1, f32[32,1,4,256]{3,2,1,0:T(4,128)} %sec_in.1, f32[3,1,4,256]{3,2,1,0:T(4,128)} %pos_in.1, ...), custom_call_target="tpu_custom_call" | custom-call | tf_op jit(solution)/shard_map/tumour_step/pallas_call | solution.py:507
  48.8 2.1 %deliver.1 = (f32[32,4,16,128]{3,2,1,0:T(8,128)}, f32[3,1,4,256]{3,2,1,0:T(4,128)}, f32[35,8,128]{2,1,0:T(8,128)}) custom-call(f32[32,4,16,128]{3,2,1,0:T(8,128)} %get-tuple-element.9.field_ref, f32[3,1,4,256]{3,2,1,0:T(4,128)} %get-tuple-element.10.disp_ref, f32[35,8,128]{2,1,0:T(8,128)} %get-tuple-element.11.arrived_ref), custom_call_target="tpu_custom_call" | custom-call | tf_op jit(solution)/shard_map/deliver/pallas_call | solution.py:563
